TPU v7x, 256 devices: a whole 4x4x8 slice. The times are simulated.
256 devices in a mesh: seq: 16 (over z, core), expert: 16 (over y, x).
Axes of the slice: x: 4, y: 4, z: 8, core: 2. Of those that a mesh axis runs over, the one named last changes fastest.
Arguments:
- queries: bfloat16 [16, 2048, 4096], P('expert', 'seq')
- new_kv: bfloat16 [16, 2048, 2, 512], P('expert', 'seq'), may hold values from -6 to 6
- kv_pool: bfloat16 [8192, 8, 2, 512], P(('seq', 'expert')), may hold values from -6 to 6
- holders: int32 [16, 256], P('expert', 'seq'), may hold values from 0 to 15, as said below
- slots: int32 [16, 256], P('expert', 'seq'), may hold values from 0 to 31
- lengths: int32 [16], replicated, may hold values from 512 to 2048, as said below
- ssm_input: bfloat16 [16, 2048, 8192], P('expert', 'seq'), may hold values from -6 to 6
- step_sizes: float32 [16, 2048, 128], P('expert', 'seq'), may hold values from 0.3 to 2
- projections: float32 [16, 2048, 32], P('expert', 'seq'), may hold values from -1 to 1
- decay_rates: float32 [128], replicated, may hold values from 4.8828126e-05 to 0.05
- skip_gain: float32 [128], replicated, may hold values from 0.5 to 1.5
- init_state: float32 [16, 128, 1024], P('expert'), may hold values from -12 to 12
Outputs:
- attended: bfloat16 [16, 2048, 4096], P('expert', 'seq')
- ssm_out: bfloat16 [16, 2048, 8192], P('expert', 'seq')
Inputs may be any that keep to these rules, and one draw needn't show every extreme that they name: `holders`: among the 16 blocks of one session on one index of seq no holder is named more than 2 times, and one holder exactly 2 times. `lengths`: in every draw one session holds exactly 2048 cached positions.
All inputs are finite; a program needn't handle non-finite values.
Results may differ from a plain program's by a relative error of at most 0.009.
Values may be sent and summed in bfloat16 or wider, within the bound.
A program may use at most 128 MiB of HBM per device.

v0:
```python
import jax
import jax.numpy as jnp
from jax import lax
from jax.sharding import PartitionSpec as P

Q_HEADS = 32
KV_HEADS = 4
HEAD_DIM = 128
CAP = 2


masked_score = -1e30


def carried_in(array, axis, combine, identity):
    devices, here = (lax.axis_size(axis), lax.axis_index(axis))
    everything = jax.tree.map(
        lambda part, kind: lax.all_gather(part.astype(kind), axis),
        array,
        (jnp.bfloat16, jnp.bfloat16),
    )
    start = jax.tree.map(
        lambda part, zero: jnp.broadcast_to(jnp.asarray(zero, part.dtype), part.shape),
        array,
        identity,
    )

    def step(k, before):
        reached = k < here
        new = combine(
            before, jax.tree.map(lambda part, own: part[k].astype(own.dtype), everything, array)
        )
        return jax.tree.map(lambda a, b: jnp.where(reached, a, b), new, before)

    return lax.fori_loop(0, devices, step, start)


def attend_block(running, key_block, visible, grouped):
    row_peak, totals, summed = running
    kv_heads = grouped.shape[1]
    head_depth = grouped.shape[3]
    key_count = key_block.shape[0]
    key_rows = key_block[:, 0].reshape(key_count, kv_heads, head_depth)
    value_rows = key_block[:, 1].reshape(key_count, kv_heads, head_depth)
    scores = jnp.einsum(
        "tkgd,skd->tkgs", grouped, key_rows, preferred_element_type=jnp.float32
    ) * head_depth ** (-0.5)
    shown_mask = visible[:, None, None, :]
    new_peak = jnp.maximum(row_peak, jnp.max(jnp.where(shown_mask, scores, masked_score), axis=-1))
    weights = jnp.where(shown_mask, jnp.exp(scores - new_peak[..., None]), 0.0)
    factor = jnp.exp(row_peak - new_peak)
    totals = totals * factor + jnp.sum(weights, axis=-1)
    summed = summed * factor[..., None] + jnp.einsum(
        "tkgs,skd->tkgd",
        weights.astype(jnp.bfloat16),
        value_rows,
        preferred_element_type=jnp.float32,
    )
    return (new_peak, totals, summed)


def sweep(running, key_piece, shard_rows, grouped, visible_rule):
    row_count = key_piece.shape[0]
    shard_count = row_count // shard_rows
    group_size = max(1, 1024 // shard_rows)
    while shard_count % group_size:
        group_size -= 1
    span_rows = shard_rows * group_size

    def advance(block_number, held_state):
        offset = block_number * span_rows
        key_block = lax.dynamic_slice_in_dim(key_piece, offset, span_rows, 0)
        key_index = offset + jnp.arange(span_rows, dtype=jnp.int32)
        visible = visible_rule(key_index)
        return attend_block(held_state, key_block, visible, grouped)

    return lax.fori_loop(0, row_count // span_rows, advance, running)


def ssm_local(inputs, step_rows, write_rows, read_rows, decay_rates):
    row_count = inputs.shape[0]
    running_log = jnp.cumsum(-step_rows * decay_rates[None, :], axis=0)
    block_decay = running_log[-1]
    affinity = jnp.dot(read_rows, write_rows.T, precision=lax.Precision.HIGHEST)
    gaps = running_log[:, None, :] - running_log[None, :, :]
    causal = (
        jnp.arange(row_count, dtype=jnp.int32)[:, None]
        >= jnp.arange(row_count, dtype=jnp.int32)[None, :]
    )[:, :, None]
    decays = jnp.where(causal, jnp.exp(jnp.minimum(gaps, 0.0)), 0.0)
    mixing = (affinity[:, :, None] * decays * step_rows[None, :, :]).astype(jnp.bfloat16)
    to_end = jnp.exp(block_decay[None, :] - running_log) * step_rows
    feeding = (to_end[:, :, None] * write_rows[:, None, :]).astype(jnp.bfloat16)
    return (running_log, block_decay, feeding, mixing)


def chain_join(earlier, later):
    return (earlier[0] + later[0], jnp.exp(later[0])[:, None] * earlier[1] + later[1])


def local(
    queries,
    new_kv,
    kv_pool,
    holders,
    slots,
    lengths,
    ssm_input,
    step_sizes,
    projections,
    decay_rates,
    skip_gain,
    init_state,
):
    owners = lax.axis_size("expert")
    holder = holders[0]
    slot_ids = slots[0]
    owner_ids = jnp.arange(owners, dtype=jnp.int32)
    onehot = (holder[:, None] == owner_ids[None, :]).astype(jnp.int32)
    before = jnp.cumsum(onehot, axis=0) - onehot
    rank_ids = jnp.sum(before * onehot, axis=1)
    placing = onehot[:, :, None] * (
        rank_ids[:, None, None] == jnp.arange(CAP, dtype=jnp.int32)[None, None, :]
    ).astype(jnp.int32)
    requests = jnp.sum(placing * (slot_ids[:, None, None] + 1), axis=0) - 1
    asked_ids = lax.all_to_all(requests, "expert", split_axis=0, concat_axis=0, tiled=True)
    safe_ids = jnp.clip(asked_ids, 0, kv_pool.shape[0] - 1)
    picked = jnp.where(
        (asked_ids >= 0)[:, :, None, None, None], kv_pool[safe_ids], jnp.zeros((), kv_pool.dtype)
    )
    arrived = lax.all_to_all(picked, "expert", split_axis=0, concat_axis=0, tiled=True)
    kv_width = kv_pool.shape[-1]
    flattened = arrived.reshape(-1, arrived.shape[2], 2, kv_width)
    context = flattened[holder * CAP + rank_ids].reshape(-1, 2, kv_width)
    token_count = queries.shape[1]
    context_rows = context.shape[0]
    group_size = Q_HEADS // KV_HEADS
    grouped = queries[0].reshape(token_count, KV_HEADS, group_size, HEAD_DIM)
    seq_index = lax.axis_index("seq")
    positions = seq_index * token_count + jnp.arange(token_count, dtype=jnp.int32)
    length = lengths[lax.axis_index("expert")]
    running = (
        jnp.full((token_count, KV_HEADS, group_size), masked_score, jnp.float32),
        jnp.zeros((token_count, KV_HEADS, group_size), jnp.float32),
        jnp.zeros((token_count, KV_HEADS, group_size, HEAD_DIM), jnp.float32),
    )
    fresh_kv = new_kv[0]

    def context_visible(key_index):
        return jnp.broadcast_to((key_index < length)[None, :], (token_count, key_index.shape[0]))

    def tail_visible(key_index):
        return key_index[None, :] <= positions[:, None]

    running = sweep(
        running,
        lax.all_gather(context, "seq", axis=0, tiled=True),
        context_rows,
        grouped,
        context_visible,
    )
    running = sweep(
        running,
        lax.all_gather(fresh_kv, "seq", axis=0, tiled=True),
        token_count,
        grouped,
        tail_visible,
    )
    row_peak, totals, summed = running
    attended = (summed / totals[..., None]).reshape(token_count, -1).astype(jnp.bfloat16)[None]
    inputs = ssm_input[0]
    state_size = projections.shape[2] // 2
    write_rows = projections[0][:, :state_size]
    read_rows = projections[0][:, state_size:]
    running_log, block_decay, feeding, mixing = ssm_local(
        inputs, step_sizes[0], write_rows, read_rows, decay_rates
    )
    head_count = decay_rates.shape[0]
    inner = inputs.reshape(token_count, head_count, -1)
    block_end = jnp.einsum(
        "shp,shn->hpn", inner, feeding, preferred_element_type=jnp.float32
    ).reshape(head_count, -1)
    inside = jnp.einsum("tsh,shp->thp", mixing, inner, preferred_element_type=jnp.float32)
    identity = (jnp.zeros_like(block_decay), jnp.zeros_like(block_end))
    decay_before, state_before = carried_in((block_decay, block_end), "seq", chain_join, identity)
    carried = jnp.exp(decay_before)[:, None] * init_state[0] + state_before
    outside = jnp.exp(running_log)[:, :, None] * jnp.einsum(
        "hpn,tn->thp",
        carried.reshape(head_count, -1, state_size),
        read_rows,
        precision=lax.Precision.HIGHEST,
    )
    ssm_out = (
        (inside + outside + skip_gain[None, :, None] * inner.astype(jnp.float32))
        .reshape(token_count, -1)
        .astype(jnp.bfloat16)[None]
    )
    return (attended, ssm_out)


def solution(mesh):
    placed = (
        P("expert", "seq", None),
        P("expert", "seq", None, None),
        P(("seq", "expert"), None, None, None),
        P("expert", "seq"),
        P("expert", "seq"),
        P(),
        P("expert", "seq", None),
        P("expert", "seq", None),
        P("expert", "seq", None),
        P(),
        P(),
        P("expert", None, None),
    )
    return jax.shard_map(
        local,
        mesh=mesh,
        in_specs=placed,
        out_specs=(P("expert", "seq", None), P("expert", "seq", None)),
        check_vma=False,
    )
```

profile of v0, /device:TPU:1, one launch (start us, length us, event | category | flops | bytes accessed | tf_op | source)
XLA Modules:
  0.0 257.9 jit_solution(1490435018404957601)
XLA Ops:
  7.2 0.9 negate_multiply_fusion
  8.3 0.9 fusion.50
  9.3 3.2 %copy.133 = bf16[1,128,8192]{1,2,0:T(8,128)(2,1)S(1)} copy(bf16[1,128,8192]{2,1,0:T(8,128)(2,1)} %param.24) | data formatting | bytes 4194304 | tf_op args[6]
  12.6 1.2 fusion.38
  14.4 0.9 copy.137
  15.2 0.8 fusion.43
  16.0 0.8 select_reduce_fusion
  17.7 13.8 %all_to_all.11 = s32[16,1,2]{2,1,0:T(1,128)S(1)} all-to-all(s32[16,1,2]{2,1,0:T(1,128)S(1)} %copy.117), channel_id=1, replica_groups=mesh['seq'=16,'expert'=16] {'expert'}, dimensions={0} | all-to-all | bytes 256 | tf_op jit(solution)/shard_map/all_to_all | solution.py:126
  33.1 1.7 gather_fusion
  34.8 1.6 copy_select_fusion
  36.4 3.7 %all-to-all-start.1 = ((bf16[16,2,8,2,512]{4,2,3,1,0:T(8,128)(2,1)}), bf16[16,2,8,2,512]{4,2,3,1,0:T(8,128)(2,1)S(1)}, u32[]{:S(2)}, u32[]{:S(2)}) async-start(bf16[16,2,8,2,512]{4,2,3,1,0:T(8,128)(2,1)} %copy_select_fusion), calls=%async_computation.1 | async-start | bytes 1048576 | tf_op jit(solution)/shard_map/all_to_all | solution.py:131
  40.1 0.7 fusion.47
  40.8 8.7 %all-to-all-done.1 = bf16[16,2,8,2,512]{4,2,3,1,0:T(8,128)(2,1)S(1)} async-done(((bf16[16,2,8,2,512]{4,2,3,1,0:T(8,128)(2,1)}), bf16[16,2,8,2,512]{4,2,3,1,0:T(8,128)(2,1)S(1)}, u32[]{:S(2)}, u32[]{:S(2)}) %all-to-all-start.1) | async-done | bytes 524320 | tf_op jit(solution)/shard_map/all_to_all | solution.py:131
  50.1 0.7 copy.160
  50.9 0.9 copy.127
  52.3 1.6 copy.124
  54.7 22.7 %all-gather.1 = bf16[16,1,128]{2,1,0:T(2,128)(2,1)S(1)} all-gather(bf16[1,1,128]{2,1,0:T(2,128)(2,1)S(1)} %convert_bitcast_fusion), channel_id=1, replica_groups=mesh['seq'=16,'expert'=16] {'seq'}, dimensions={0}, use_global_device_ids=true | all-gather | bytes 4352 | tf_op jit(solution)/shard_map/all_gather | solution.py:18
  77.3 1.2 copy.138
  79.4 6.3 %fusion.28 = f32[128,128,64]{1,2,0:T(8,128)} fusion(bf16[128,128,64]{0,2,1:T(8,128)(2,1)} %bitcast.180, f32[128,128]{0,1:T(8,128)S(1)} %copy.132, f32[128,128]{0,1:T(8,128)S(1)} %copy.130, f32[128,128]{1,0:T(8,128)S(1)} %fusion.45, pred[128,128]{1,0:T(8,128)(4,1)S(1)} %iota_compare_fusion), kind=kOutput, calls=%fused_computation.49 | convolution fusion | flops 281018368 | bytes 6504448 | tf_op jit(solution)/shard_map/tsh,shp->thp/dot_general | solution.py:183
  85.7 18.3 %while.54 = (s32[]{:T(128)}, f32[128]{0:T(128)S(1)}, f32[128,1024]{1,0:T(8,128)S(1)}, s32[]{:T(128)}, bf16[16,128]{1,0:T(8,128)(2,1)S(1)}, /*index=5*/bf16[16,128,1024]{2,1,0:T(8,128)(2,1)}, s32[]{:T(128)}, s32[]{:T(128)}) while((s32[]{:T(128)}, f32[128]{0:T(128)S(1)}, f32[128,1024]{1,0:T(8,128)S(1)}, s32[]{:T(128)}, ...), condition=%wide.region_13.14_spmd.clone, body=%wide.region_12.13_spmd.clone.sunk | while | flops 655876 | bytes 1313139 | solution.py:35
  85.7 1.1 fusion.87
  86.9 1.1 fusion.87
  88.0 1.1 fusion.87
  89.1 1.1 fusion.87
  90.3 1.1 fusion.87
  91.4 1.1 fusion.87
  92.6 1.1 fusion.87
  93.7 1.1 fusion.87
  94.9 1.1 fusion.87
  96.0 1.1 fusion.87
  97.2 1.1 fusion.87
  98.3 1.1 fusion.87
  99.4 1.1 fusion.87
  100.6 1.1 fusion.87
  101.7 1.1 fusion.87
  102.9 1.1 fusion.87
  104.8 10.4 %fusion.31 = bf16[128,128,64]{0,2,1:T(8,128)(2,1)} fusion(f32[128,128,64]{1,2,0:T(8,128)} %fusion.28, bf16[128,128,64]{0,2,1:T(8,128)(2,1)} %bitcast.181, f32[128,64,16]{1,2,0:T(8,128)S(1)} %copy.140, f32[128]{0:T(128)S(1)} %copy-done.6, f32[128,128]{0,1:T(8,128)S(1)} %copy.134, f32[128,32]{0,1:T(8,128)S(1)} %bitcast.193), kind=kOutput, calls=%fused_computation.53 | convolution fusion | flops 207618048 | bytes 9511424 | tf_op jit(solution)/shard_map/hpn,tn->thp/dot_general | solution.py:187
  115.2 4.1 %copy.141 = bf16[1,128,8192]{2,1,0:T(8,128)(2,1)} copy(bf16[1,128,8192]{1,2,0:T(8,128)(2,1)} %bitcast.182) | data formatting | bytes 4194304
  119.3 70.3 %while.53 = (s32[]{:T(128)}, f32[128,4,8]{0,2,1:T(8,128)S(1)}, f32[128,4,8]{0,2,1:T(8,128)S(1)}, f32[128,4,8,128]{0,3,2,1:T(8,128)}, s32[]{:T(128)}, /*index=5*/...) while((s32[]{:T(128)}, f32[128,4,8]{0,2,1:T(8,128)S(1)}, ...), condition=%wide.region_6.7_spmd.clone, body=%wide.region_3.6_spmd.clone.sunk | while | flops 2195216384 | bytes 66326728 | solution.py:77
  119.3 2.6 %constant_dynamic-slice_fusion.8 = (bf16[1024,1,512]{2,0,1:T(8,128)(2,1)S(1)}, bf16[1024,1,512]{2,0,1:T(8,128)(2,1)}) fusion(bf16[2048,2,512]{2,0,1:T(8,128)(2,1)} %get-tuple-element.740, s32[]{:T(128)S(6)} %select_n.177, s32[]{:T(128)S(6)} %add.313), kind=kLoop, calls=%fused_computation.39.clone.1 | loop fusion | bytes 4194312 | tf_op jit(solution)/shard_map/while/body/eval_jaxpr/slice | solution.py:44
  122.0 2.3 copy.164
  124.2 0.7 add_compare_fusion.2
  124.9 9.0 %fusion.84 = (f32[128,4,8]{0,2,1:T(8,128)S(1)}, f32[4,1024,128,8]{2,1,3,0:T(8,128)}) fusion(pred[1024]{0:T(1024)(128)(4,1)S(1)} %add_compare_fusion.2, bf16[1024,4,128,1]{0,2,3,1:T(8,128)(2,1)} %bitcast.174, bf16[128,4,8,128]{3,0,2,1:T(8,128)(2,1)S(1)} %get-tuple-element.741), kind=kOutput, calls=%fused_computation.24.clone.1 | convolution fusion | flops 1086320640 | bytes 18891776 | tf_op jit(solution)/shard_map/while/body/eval_jaxpr/tkgd,skd->tkgs/dot_general | solution.py:45
  133.9 8.1 %fusion.85 = f32[128,4,8]{0,2,1:T(8,128)S(1)} fusion(f32[4,1024,128,8]{2,1,3,0:T(8,128)} %get-tuple-element.699, f32[128,4,8]{0,2,1:T(8,128)S(1)} %select_maximum_fusion.2, pred[1024]{0:T(1024)(128)(4,1)S(1)} %add_compare_fusion.2), kind=kLoop, calls=%fused_computation.28.clone.1 | loop fusion | flops 16773120 | bytes 16811008 | tf_op jit(solution)/shard_map/while/body/eval_jaxpr/reduce_sum | solution.py:52
  142.1 1.3 copy.165
  143.4 11.0 %bitcast_add_fusion.6 = f32[128,4,8,128]{0,3,2,1:T(8,128)} fusion(f32[128,4,8,128]{0,3,2,1:T(8,128)} %get-tuple-element.726, bf16[1024,4,128,1]{0,2,3,1:T(8,128)(2,1)} %bitcast.178, f32[4,1024,128,8]{2,1,3,0:T(8,128)} %get-tuple-element.699, f32[128,4,8]{0,2,1:T(8,128)S(1)} %select_maximum_fusion.2, pred[1024]{0:T(1024)(128)(4,1)S(1)} %add_compare_fusion.2, ...), kind=kOutput, calls=%fused_computation.31.clone.1 | convolution fusion | flops 1092091904 | bytes 22053888 | tf_op jit(solution)/shard_map/while/body/eval_jaxpr/tkgs,skd->tkgd/dot_general | solution.py:53
  154.4 2.6 %constant_dynamic-slice_fusion.8 = (bf16[1024,1,512]{2,0,1:T(8,128)(2,1)S(1)}, bf16[1024,1,512]{2,0,1:T(8,128)(2,1)}) fusion(bf16[2048,2,512]{2,0,1:T(8,128)(2,1)} %get-tuple-element.740, s32[]{:T(128)S(6)} %select_n.177, s32[]{:T(128)S(6)} %add.313), kind=kLoop, calls=%fused_computation.39.clone.1 | loop fusion | bytes 4194312 | tf_op jit(solution)/shard_map/while/body/eval_jaxpr/slice | solution.py:44
  157.0 2.3 copy.164
  159.3 0.7 add_compare_fusion.2
  160.0 8.9 %fusion.84 = (f32[128,4,8]{0,2,1:T(8,128)S(1)}, f32[4,1024,128,8]{2,1,3,0:T(8,128)}) fusion(pred[1024]{0:T(1024)(128)(4,1)S(1)} %add_compare_fusion.2, bf16[1024,4,128,1]{0,2,3,1:T(8,128)(2,1)} %bitcast.174, bf16[128,4,8,128]{3,0,2,1:T(8,128)(2,1)S(1)} %get-tuple-element.741), kind=kOutput, calls=%fused_computation.24.clone.1 | convolution fusion | flops 1086320640 | bytes 18891776 | tf_op jit(solution)/shard_map/while/body/eval_jaxpr/tkgd,skd->tkgs/dot_general | solution.py:45
  168.9 7.9 %fusion.85 = f32[128,4,8]{0,2,1:T(8,128)S(1)} fusion(f32[4,1024,128,8]{2,1,3,0:T(8,128)} %get-tuple-element.699, f32[128,4,8]{0,2,1:T(8,128)S(1)} %select_maximum_fusion.2, pred[1024]{0:T(1024)(128)(4,1)S(1)} %add_compare_fusion.2), kind=kLoop, calls=%fused_computation.28.clone.1 | loop fusion | flops 16773120 | bytes 16811008 | tf_op jit(solution)/shard_map/while/body/eval_jaxpr/reduce_sum | solution.py:52
  176.8 1.3 copy.165
  178.1 11.4 %bitcast_add_fusion.6 = f32[128,4,8,128]{0,3,2,1:T(8,128)} fusion(f32[128,4,8,128]{0,3,2,1:T(8,128)} %get-tuple-element.726, bf16[1024,4,128,1]{0,2,3,1:T(8,128)(2,1)} %bitcast.178, f32[4,1024,128,8]{2,1,3,0:T(8,128)} %get-tuple-element.699, f32[128,4,8]{0,2,1:T(8,128)S(1)} %select_maximum_fusion.2, pred[1024]{0:T(1024)(128)(4,1)S(1)} %add_compare_fusion.2, ...), kind=kOutput, calls=%fused_computation.31.clone.1 | convolution fusion | flops 1092091904 | bytes 22053888 | tf_op jit(solution)/shard_map/while/body/eval_jaxpr/tkgs,skd->tkgd/dot_general | solution.py:53
  189.6 58.5 %while.52 = (s32[]{:T(128)}, f32[128,4,8]{0,2,1:T(8,128)S(1)}, f32[128,4,8]{0,2,1:T(8,128)S(1)}, f32[128,4,8,128]{0,3,2,1:T(8,128)}, bf16[2048,2,512]{0,2,1:T(8,...) while((s32[]{:T(128)}, f32[128,4,8]{0,2,1:T(8,128)S(1)}, ...), condition=%wide.region_10.11_spmd.clone, body=%wide.region_7.10_spmd.clone.sunk | while | flops 2194809856 | bytes 62661824 | solution.py:77
  189.6 1.7 constant_dynamic-slice_fusion.7
  191.5 7.2 %fusion.78 = (f32[128,4,8]{0,2,1:T(8,128)S(1)}, f32[4,1024,128,8]{2,1,3,0:T(8,128)}) fusion(pred[128,1024]{0,1:T(8,128)(4,1)S(1)} %broadcast_compare_fusion.2, bf16[1024,4,128,1]{0,2,3,1:T(8,128)(2,1)S(1)} %bitcast.175, bf16[128,4,8,128]{3,0,2,1:T(8,128)(2,1)S(1)} %get-tuple-element.776), kind=kOutput, calls=%fused_computation.5.clone.1 | convolution fusion | flops 1086320640 | bytes 19021824 | tf_op jit(solution)/shard_map/while/body/eval_jaxpr/tkgd,skd->tkgs/dot_general | solution.py:45
  198.7 9.1 %fusion.79 = f32[128,4,8]{0,2,1:T(8,128)S(1)} fusion(f32[4,1024,128,8]{2,1,3,0:T(8,128)} %get-tuple-element.686, f32[128,4,8]{0,2,1:T(8,128)S(1)} %max.23, pred[128,1024]{0,1:T(8,128)(4,1)S(1)} %broadcast_compare_fusion.2), kind=kLoop, calls=%fused_computation.9.clone.1 | loop fusion | flops 16773120 | bytes 16941056 | tf_op jit(solution)/shard_map/while/body/eval_jaxpr/reduce_sum | solution.py:52
  207.8 11.0 %bitcast_add_fusion.5 = f32[128,4,8,128]{0,3,2,1:T(8,128)} fusion(f32[128,4,8,128]{0,3,2,1:T(8,128)} %get-tuple-element.762, bf16[1024,4,128,1]{0,2,3,1:T(8,128)(2,1)S(1)} %bitcast.176, f32[4,1024,128,8]{2,1,3,0:T(8,128)} %get-tuple-element.686, f32[128,4,8]{0,2,1:T(8,128)S(1)} %max.23, pred[128,1024]{0,1:T(8,128)(4,1)S(1)} %broadcast_compare_fusion.2, ...), kind=kOutput, calls=%fused_computation.12.clone.1 | convolution fusion | flops 1091567616 | bytes 22183936 | tf_op jit(solution)/shard_map/while/body/eval_jaxpr/tkgs,skd->tkgd/dot_general | solution.py:53
  218.8 1.7 constant_dynamic-slice_fusion.7
  220.8 7.2 %fusion.78 = (f32[128,4,8]{0,2,1:T(8,128)S(1)}, f32[4,1024,128,8]{2,1,3,0:T(8,128)}) fusion(pred[128,1024]{0,1:T(8,128)(4,1)S(1)} %broadcast_compare_fusion.2, bf16[1024,4,128,1]{0,2,3,1:T(8,128)(2,1)S(1)} %bitcast.175, bf16[128,4,8,128]{3,0,2,1:T(8,128)(2,1)S(1)} %get-tuple-element.776), kind=kOutput, calls=%fused_computation.5.clone.1 | convolution fusion | flops 1086320640 | bytes 19021824 | tf_op jit(solution)/shard_map/while/body/eval_jaxpr/tkgd,skd->tkgs/dot_general | solution.py:45
  228.0 9.1 %fusion.79 = f32[128,4,8]{0,2,1:T(8,128)S(1)} fusion(f32[4,1024,128,8]{2,1,3,0:T(8,128)} %get-tuple-element.686, f32[128,4,8]{0,2,1:T(8,128)S(1)} %max.23, pred[128,1024]{0,1:T(8,128)(4,1)S(1)} %broadcast_compare_fusion.2), kind=kLoop, calls=%fused_computation.9.clone.1 | loop fusion | flops 16773120 | bytes 16941056 | tf_op jit(solution)/shard_map/while/body/eval_jaxpr/reduce_sum | solution.py:52
  237.1 11.0 %bitcast_add_fusion.5 = f32[128,4,8,128]{0,3,2,1:T(8,128)} fusion(f32[128,4,8,128]{0,3,2,1:T(8,128)} %get-tuple-element.762, bf16[1024,4,128,1]{0,2,3,1:T(8,128)(2,1)S(1)} %bitcast.176, f32[4,1024,128,8]{2,1,3,0:T(8,128)} %get-tuple-element.686, f32[128,4,8]{0,2,1:T(8,128)S(1)} %max.23, pred[128,1024]{0,1:T(8,128)(4,1)S(1)} %broadcast_compare_fusion.2, ...), kind=kOutput, calls=%fused_computation.12.clone.1 | convolution fusion | flops 1091567616 | bytes 22183936 | tf_op jit(solution)/shard_map/while/body/eval_jaxpr/tkgs,skd->tkgd/dot_general | solution.py:53
  248.1 1.9 divide_convert_fusion
  250.0 1.3 copy.148
  (99 shorter events, 7.7 us)
Async XLA Ops:
  7.2 25.9 %copy-start = (bf16[32,8,2,512]{3,2,1,0:T(2,128)(2,1)S(1)}, bf16[32,8,2,512]{3,2,1,0:T(2,128)(2,1)}, u32[]{:S(2)}) copy-start(bf16[32,8,2,512]{3,2,1,0:T(2,128)(2,1)} %param.20) | copy-start | bytes 1572868
  7.2 5.4 %copy-start.5 = (f32[1,128,32]{1,2,0:T(8,128)S(1)}, f32[1,128,32]{1,2,0:T(8,128)}, u32[]{:S(2)}) copy-start(f32[1,128,32]{1,2,0:T(8,128)} %param.26) | copy-start | bytes 49156
  7.2 78.5 %all-gather.8.cloned.1.call-start = ((), (), s32[]{:S(2)}) async-start(), calls=%async_computation.3 | async-start | bytes 4456448 | tf_op jit(solution)/shard_map/all_gather | solution.py:18
  12.5 38.3 %copy-start.2 = (bf16[1,128,8192]{1,2,0:T(8,128)(2,1)}, bf16[1,128,8192]{1,2,0:T(8,128)(2,1)S(1)}, u32[]{:S(2)}) copy-start(bf16[1,128,8192]{1,2,0:T(8,128)(2,1)S(1)} %copy.133) | copy-start | bytes 6291460
  15.2 35.7 %copy-start.4 = (bf16[1,128,2,512]{3,2,1,0:T(2,128)(2,1)S(1)}, bf16[1,128,2,512]{3,2,1,0:T(2,128)(2,1)}, u32[]{:S(2)}) copy-start(bf16[1,128,2,512]{3,2,1,0:T(2,128)(2,1)} %param.19) | copy-start | bytes 786436
  16.9 0.9 copy-start.7
  36.4 42.2 %copy-start.3 = (f32[1,128,128]{2,1,0:T(8,128)S(1)}, f32[1,128,128]{2,1,0:T(8,128)}, u32[]{:S(2)}) copy-start(f32[1,128,128]{2,1,0:T(8,128)} %param.25) | copy-start | bytes 196612
  36.4 13.2 %all-to-all-start.1 = ((bf16[16,2,8,2,512]{4,2,3,1,0:T(8,128)(2,1)}), bf16[16,2,8,2,512]{4,2,3,1,0:T(8,128)(2,1)S(1)}, u32[]{:S(2)}, u32[]{:S(2)}) async-start(bf16[16,2,8,2,512]{4,2,3,1,0:T(8,128)(2,1)} %copy_select_fusion), calls=%async_computation.1 | async-start | bytes 1048576 | tf_op jit(solution)/shard_map/all_to_all | solution.py:131
  40.1 38.7 %copy-start.8 = (s32[16]{0:T(128)S(1)}, s32[16]{0:T(128)}, u32[]{:S(2)}) copy-start(s32[16]{0:T(128)} %param.23) | copy-start | bytes 196
  40.1 79.2 %all-gather.6.cloned.1.call-start = ((), (), s32[]{:S(2)}) async-start(), calls=%async_computation.2 | async-start | bytes 4456448 | tf_op jit(solution)/shard_map/all_gather | solution.py:157
  50.9 138.7 %all-gather.10.cloned.1.call-start = ((), (), s32[]{:S(2)}) async-start(), calls=%async_computation.4 | async-start | bytes 4456448 | tf_op jit(solution)/shard_map/all_gather | solution.py:164
  85.7 19.1 %copy-start.6 = (f32[128]{0:T(128)S(1)}, f32[128]{0:T(128)}, u32[]{:S(2)}) copy-start(f32[128]{0:T(128)} %param.28) | copy-start | bytes 1540
  248.1 3.2 %copy-start.1 = (bf16[32,8,2,512]{3,2,1,0:T(2,128)(2,1)S(1)}, bf16[32,8,2,512]{3,2,1,0:T(2,128)(2,1)}, u32[]{:S(2)}) copy-start(bf16[32,8,2,512]{3,2,1,0:T(2,128)(2,1)} %param.20) | copy-start | bytes 1572868
Sparse Core Ops, SparseCore 0:
  15.4 46.3 all-gather.7
  64.2 41.0 all-gather.5
  107.0 47.8 all-gather.9
where the time goes:
time: 260 us; the launch traced here: 258 us
  matrix products  94.8 us (36%)
  other arithmetic  63.2 us (24%)
  blocking collectives  36.4 us (14%)
  local copies, waits for them, and re-layouts  36.3 us (14%)
  between operations  14.1 us (5%)
  waiting for transfers between devices  8.78 us (3%)
  starting transfers between devices  3.83 us (1%)
    dot_general x4, matrix products, attend_block(): jnp.einsum('tkgs,skd->tkgd', weights.astype(jnp.bfloat16), value_rows, pr...  44.4 us
    reduce_sum x4, other arithmetic, attend_block(): totals = totals * factor + jnp.sum(weights, axis=-1)  34.2 us
    dot_general x4, matrix products, attend_block(): jnp.einsum('tkgd,skd->tkgs', grouped, key_rows, preferred_element_type=jn...  32.3 us
    all_gather x1, blocking collectives, carried_in(): lax.all_gather(part.astype(kind), axis)  22.7 us
    select_n x16, other arithmetic, step(): return jax.tree.map(lambda a, b: jnp.where(reached, a, b), new, before)  17.5 us
    all_to_all x1, blocking collectives, local(): lax.all_to_all(requests, 'expert', split_axis=0, concat_axis=0, tiled=True)  13.8 us
    unnamed x26, local copies, waits for them, and re-layouts  11.8 us
    dot_general x1, matrix products, local(): jnp.einsum('hpn,tn->thp', carried.reshape(head_count, -1, state_size), re...  10.4 us
  transfers between devices with their start and end apart: 4, of which 1 were waited for; matrix products, arithmetic and copies ran while one was open for 48% of the time, Pallas kernels for 0%

commit v1 on v0

v1 whole, which is shorter than its diff:
```python
import functools

import jax
import jax.numpy as jnp
from jax import lax
from jax.experimental import pallas as pl
from jax.experimental.pallas import tpu as pltpu
from jax.sharding import PartitionSpec as P

MESH = pl.DeviceIdType.MESH
BF = jnp.bfloat16
F32 = jnp.float32
I32 = jnp.int32
HIGH = lax.Precision.HIGHEST

KVH = 4
GRP = 8
DIM = 128
TOK = 128
NZ = 8
NEX = 16
UNIT = 256
HALF = 64
STATE = 16
CH = 8192
HCH = CH // 2
NSUB = 2
SUB = HCH // NSUB
SCALE = (DIM ** -0.5) * 1.4426950408889634
LOW = -1e30


def iota(shape, axis):
    return lax.broadcasted_iota(I32, shape, axis)


def kernel(
    q_ref, kv_ref, pool_ref, hold_ref, slot_ref, len_ref,
    x_ref, step_ref, proj_ref, decay_ref, skip_ref, init_ref,
    att_ref, ssm_ref,
    buf, qs, peak, acc, reqs, ids, picked, arrived, compact,
    xw, gain, dexp, sexp, ends, amat, plo,
    e_out, e_in, d_in, p_in, p_out, c_sib, c_in, carried,
    ksend, krecv, isend, irecv, bsend, brecv, esend, erecv, psend, precv, csend, crecv,
):
    me = lax.axis_index("seq")
    ex = lax.axis_index("expert")
    z = me // 2
    c = lax.rem(me, 2)
    right = lax.rem(z + 1, NZ) * 2 + c
    left = lax.rem(z + NZ - 1, NZ) * 2 + c
    sib = z * 2 + 1 - c

    barrier = pltpu.get_barrier_semaphore()
    for d in (right, left, sib):
        pl.semaphore_signal(barrier, inc=1, device_id=(d, ex), device_id_type=MESH)

    def greet(k, _):
        pl.semaphore_signal(
            barrier, inc=1, device_id=(me, lax.rem(ex + k, NEX)), device_id_type=MESH
        )
        return 0

    lax.fori_loop(1, NEX, greet, 0)

    spread = (iota((16, 128), 1) // 8 == iota((16, 128), 0)).astype(F32)
    hold = jnp.dot(hold_ref[...].astype(F32), spread, preferred_element_type=F32)
    slot = jnp.dot(slot_ref[...].astype(F32), spread, preferred_element_type=F32)
    row = iota((256, 128), 0)
    lane = iota((256, 128), 1)
    named = (hold[0:1] == (row // 16).astype(F32)).astype(F32)
    lead = ((iota((128, 128), 0) // 8 < iota((128, 128), 1) // 8)
            & (lax.rem(iota((128, 128), 0), 8) == 0)).astype(BF)
    before = jnp.dot(named.astype(BF), lead, preferred_element_type=F32)
    chosen = named * (before == lax.rem(row // 8, 2).astype(F32)).astype(F32)
    first = (lax.rem(lane, 8) == 0).astype(F32)
    wanted = jnp.sum(chosen * first * slot[0:1], axis=1, keepdims=True)
    reqs[...] = jnp.broadcast_to(wanted, (256, 128)).astype(I32)
    place = chosen * (lax.rem(row, 8) == lax.rem(lane, 8)).astype(F32)
    compact[...] = place.T.astype(BF)

    def where_rows(array, origin, half):
        return pl.ds(pl.multiple_of((array * 16 + origin) * TOK + half * HALF, HALF), HALF)

    def kv_copy(array, kind, s, half, origin, to):
        k = ((array * 4 + kind) * 5 + s) * 2 + half
        ref = buf.at[where_rows(array, origin, half)]
        return pltpu.make_async_remote_copy(
            src_ref=ref, dst_ref=ref, send_sem=ksend.at[k], recv_sem=krecv.at[k],
            device_id=(to, ex), device_id_type=MESH,
        )

    def right_origin(s):
        return lax.rem(z + NZ - s, NZ) * 2

    def left_origin(s):
        return lax.rem(z + s, NZ) * 2

    def send_own(array):
        for half in range(2):
            kv_copy(array, 0, 1, half, me, right).start()
            kv_copy(array, 1, 1, half, me, left).start()
        for half in range(2):
            kv_copy(array, 2, 0, half, me, sib).start()

    buf[where_rows(0, me, 0)] = kv_ref[0:HALF]
    buf[where_rows(0, me, 1)] = kv_ref[HALF:TOK]

    pl.semaphore_wait(barrier, 18)
    send_own(0)

    def ask(k, _):
        to = lax.rem(ex + k, NEX)
        pltpu.make_async_remote_copy(
            src_ref=reqs.at[pl.ds(pl.multiple_of(to * 16, 16), 16)],
            dst_ref=ids.at[pl.ds(pl.multiple_of(ex * 16, 16), 16)],
            send_sem=isend.at[k], recv_sem=irecv.at[k],
            device_id=(me, to), device_id_type=MESH,
        ).start()
        return 0

    lax.fori_loop(1, NEX, ask, 0)
    mine = pl.ds(pl.multiple_of(ex * 16, 16), 16)
    ids[mine] = reqs[mine]

    dec = decay_ref[...]
    steps = step_ref[...]
    lower = iota((128, 128), 0) >= iota((128, 128), 1)
    logs = jnp.dot(lower.astype(F32), -steps * dec, precision=HIGH, preferred_element_type=F32)
    total = logs[127:128]
    rows = jnp.concatenate(
        [
            jnp.exp(total - logs) * steps,
            jnp.exp(logs - total),
            jnp.broadcast_to(jnp.exp(total), (8, 128)),
            jnp.broadcast_to(skip_ref[...], (8, 128)),
        ],
        axis=0,
    )
    rows_hi = rows.astype(BF)
    rows_lo = (rows - rows_hi.astype(F32)).astype(BF)
    proj = proj_ref[...]
    proj_t = proj.T
    write_t = jnp.concatenate([jnp.zeros((STATE, 128), F32), proj_t[0:STATE]], axis=0)
    affinity = jnp.dot(proj, write_t, precision=HIGH, preferred_element_type=F32)
    amat[...] = jnp.where(lower, affinity, 0.0).astype(BF)
    plo[0] = proj.astype(BF)
    plo[1] = (proj - proj.astype(BF).astype(F32)).astype(BF)
    pt_hi = proj_t.astype(BF)
    pt_lo = (proj_t - pt_hi.astype(F32)).astype(BF)

    def widen(n, _):
        cols = pl.ds(pl.multiple_of(n * 256, 256), 256)
        one = (iota((128, 256), 0) == n * 4 + iota((128, 256), 1) // 64).astype(BF)
        wide = jnp.dot(rows_hi, one, preferred_element_type=F32) + jnp.dot(
            rows_lo, one, preferred_element_type=F32
        )
        fed = (x_ref[:, cols].astype(F32) * wide[0:128]).astype(BF)
        xw[:, cols] = fed
        gain[:, cols] = wide[128:256]
        dexp[:, cols] = wide[256:264]
        sexp[:, cols] = wide[264:272]
        end = jnp.dot(pt_hi, fed, preferred_element_type=F32) + jnp.dot(
            pt_lo, fed, preferred_element_type=F32
        )
        ends[:, cols] = end[0:STATE]
        return 0

    lax.fori_loop(0, CH // 256, widen, 0)

    my_half = pl.ds(pl.multiple_of(c * HCH, HCH), HCH)
    sib_half = pl.ds(pl.multiple_of((1 - c) * HCH, HCH), HCH)
    e_out[...] = ends[:, sib_half].astype(BF)

    def e_copy():
        return pltpu.make_async_remote_copy(
            src_ref=e_out, dst_ref=e_in, send_sem=esend.at[0], recv_sem=erecv.at[0],
            device_id=(sib, ex), device_id_type=MESH,
        )

    def d_copy():
        return pltpu.make_async_remote_copy(
            src_ref=dexp.at[:, sib_half], dst_ref=d_in, send_sem=esend.at[1],
            recv_sem=erecv.at[1], device_id=(sib, ex), device_id_type=MESH,
        )

    e_copy().start()
    d_copy().start()

    def ask_wait(k, _):
        source = pl.ds(pl.multiple_of(lax.rem(ex + NEX - k, NEX) * 16, 16), 16)
        pltpu.make_async_remote_copy(
            src_ref=ids.at[source], dst_ref=ids.at[source],
            send_sem=isend.at[k], recv_sem=irecv.at[k],
            device_id=(me, lax.rem(ex + k, NEX)), device_id_type=MESH,
        ).wait_recv()
        return 0

    lax.fori_loop(1, NEX, ask_wait, 0)
    got = ids[...]
    same = lax.rem(row, 8) == lax.rem(lane, 8)
    pick = jnp.concatenate(
        [
            ((got == lane // 8) & same).astype(BF),
            ((got == lane // 8 + 16) & same).astype(BF),
        ],
        axis=1,
    )
    picked[...] = jnp.dot(pick, pool_ref[...], preferred_element_type=F32).astype(BF)

    def block_copy(k):
        to = lax.rem(ex + k, NEX)
        return pltpu.make_async_remote_copy(
            src_ref=picked.at[pl.ds(pl.multiple_of(to * 16, 16), 16)],
            dst_ref=arrived.at[pl.ds(pl.multiple_of(ex * 16, 16), 16)],
            send_sem=bsend.at[k], recv_sem=brecv.at[k],
            device_id=(me, to), device_id_type=MESH,
        )

    def give(k, _):
        block_copy(k).start()
        return 0

    lax.fori_loop(1, NEX, give, 0)
    arrived[mine] = picked[mine]

    for g in range(KVH):
        for j in range(GRP):
            h = g * GRP + j
            qs[g, j * TOK:(j + 1) * TOK, :] = q_ref[:, h * DIM:(h + 1) * DIM]
    peak[...] = jnp.full_like(peak, LOW)
    acc[...] = jnp.zeros_like(acc)
    length = len_ref[ex]

    def attend(start, shown, bias):
        keep = iota((UNIT, DIM), 0) < shown
        one = keep.astype(F32).astype(BF)
        for g in range(KVH):
            kcols = slice(g * DIM, (g + 1) * DIM)
            vcols = slice(512 + g * DIM, 512 + (g + 1) * DIM)
            key = buf[pl.ds(start, UNIT), kcols]
            value = buf[pl.ds(start, UNIT), vcols]
            key = jnp.where(keep, key, jnp.broadcast_to(kv_ref[0:1, kcols], (UNIT, DIM)))
            value = value * one
            score = lax.dot_general(
                qs[g], key, (((1,), (1,)), ((), ())), preferred_element_type=F32
            )
            if bias is not None:
                score = score + bias
            old = peak[g]
            new = jnp.maximum(old, jnp.max(score, axis=1, keepdims=True))
            weight = jnp.exp2((score - jnp.concatenate([new, new], 1)) * SCALE).astype(BF)
            factor = jnp.exp2((old - new) * SCALE)
            acc[g] = acc[g] * jnp.concatenate([factor, factor], 1) + jnp.dot(
                weight, jnp.concatenate([value, one], axis=1), preferred_element_type=F32
            )
            peak[g] = new

    def sib_wait(array, kind, s, half):
        if kind == 0:
            origin = right_origin(s)
        else:
            origin = left_origin(s)
        kv_copy(array, 2 + kind, s, half, origin + 1 - c, sib).wait_recv()

    for half in range(2):
        kv_copy(0, 2, 0, half, sib, sib).wait_recv()
    token = lax.rem(iota((GRP * TOK, UNIT), 0), TOK) + c * TOK
    bias = jnp.where(iota((GRP * TOK, UNIT), 1) <= token, 0.0, LOW)
    attend(pl.multiple_of(z * UNIT, UNIT), UNIT, bias)

    def p_copy(k):
        return pltpu.make_async_remote_copy(
            src_ref=p_out.at[k], dst_ref=p_in.at[k], send_sem=psend.at[k],
            recv_sem=precv.at[k], device_id=(right, ex), device_id_type=MESH,
        )

    def c_copy(k):
        return pltpu.make_async_remote_copy(
            src_ref=c_sib.at[k], dst_ref=c_in.at[k], send_sem=csend.at[k],
            recv_sem=crecv.at[k], device_id=(sib, ex), device_id_type=MESH,
        )

    def chain():
        e_copy().wait_recv()
        d_copy().wait_recv()
        for k in range(NSUB):
            cols = pl.ds(pl.multiple_of(c * HCH + k * SUB, SUB), SUB)
            piece = slice(k * SUB, (k + 1) * SUB)

            @pl.when(z > 0)
            def _():
                p_copy(k).wait_recv()
                carried[:, cols] = p_in[k].astype(F32)

            @pl.when(z == 0)
            def _():
                carried[:, cols] = init_ref[:, cols]

            entering = carried[:, cols]
            own_e, own_d = ends[:, cols], dexp[0:1, cols]
            sib_e, sib_d = e_in[:, piece].astype(F32), d_in[0:1, piece]
            even = c == 0
            e0, e1 = jnp.where(even, own_e, sib_e), jnp.where(even, sib_e, own_e)
            d0, d1 = jnp.where(even, own_d, sib_d), jnp.where(even, sib_d, own_d)
            middle = d0 * entering + e0
            p_out[k] = (d1 * middle + e1).astype(BF)

            @pl.when(z < NZ - 1)
            def _():
                p_copy(k).start()

            c_sib[k] = jnp.where(even, middle, entering).astype(BF)
            c_copy(k).start()
            carried[:, cols] = jnp.where(even, entering, middle)

    def ssm_finish():
        for k in range(NSUB):
            c_copy(k).wait_recv()
            cols = pl.ds(pl.multiple_of((1 - c) * HCH + k * SUB, SUB), SUB)
            carried[:, cols] = c_in[k].astype(F32)

        def finish(n, _):
            cols = pl.ds(pl.multiple_of(n * 256, 256), 256)
            state = (carried[:, cols] * dexp[0:1, cols]).astype(BF)
            state = jnp.concatenate([jnp.zeros((STATE, 256), BF), state], axis=0)
            mixed = (
                jnp.dot(amat[...], xw[:, cols], preferred_element_type=F32)
                + jnp.dot(plo[0], state, preferred_element_type=F32)
                + jnp.dot(plo[1], state, preferred_element_type=F32)
            )
            ssm_ref[:, cols] = (
                gain[:, cols] * mixed + sexp[0:1, cols] * x_ref[:, cols].astype(F32)
            ).astype(BF)
            return 0

        lax.fori_loop(0, CH // 256, finish, 0)

    def assemble():
        def block_wait(k, _):
            source = pl.ds(pl.multiple_of(lax.rem(ex + NEX - k, NEX) * 16, 16), 16)
            pltpu.make_async_remote_copy(
                src_ref=arrived.at[source], dst_ref=arrived.at[source],
                send_sem=bsend.at[k], recv_sem=brecv.at[k],
                device_id=(me, lax.rem(ex + k, NEX)), device_id_type=MESH,
            ).wait_recv()
            return 0

        lax.fori_loop(1, NEX, block_wait, 0)
        context = jnp.dot(compact[...], arrived[...], preferred_element_type=F32).astype(BF)
        buf[where_rows(1, me, 0)] = context[0:HALF]
        buf[where_rows(1, me, 1)] = context[HALF:TOK]
        send_own(1)

    def stage(k):
        is_ctx = (k == 3) | (k >= 5)
        s = jnp.where(k < 3, k + 1, jnp.where(k == 3, 1, jnp.where(k == 4, 4, k - 3)))
        return jnp.where(is_ctx, 1, 0), s

    turn = 1 + (3 * z) // 2

    def step(it, _):
        k = it // 2
        j = lax.rem(it, 2)
        array, s = stage(k)
        last = 4 - j

        @pl.when(it == 3)
        def _():
            assemble()

        @pl.when(s <= last)
        def _():
            for kind in range(2):
                half = j if kind == 0 else 1 - j
                origin = (right_origin(s) if kind == 0 else left_origin(s)) + c
                kv_copy(array, kind, s, half, origin, sib).wait_recv()

                @pl.when(s < last)
                def _():
                    kv_copy(array, kind, s + 1, half, origin, right if kind == 0 else left).start()

                kv_copy(array, 2 + kind, s, half, origin, sib).start()

        @pl.when(it == turn)
        def _():
            chain()

        @pl.when(it == turn + 2)
        def _():
            ssm_finish()

        parray, ps = stage(k - 1)
        own = (k - 1 == 4) & (j == 1)
        uarray = jnp.where(own, 1, parray)
        chip = jnp.where(
            own, z, lax.rem(jnp.where(j == 0, z + NZ - ps, z + ps), NZ)
        )

        @pl.when(it >= 2)
        def _():
            @pl.when(own)
            def _():
                for half in range(2):
                    kv_copy(1, 2, 0, half, sib, sib).wait_recv()

            @pl.when(jnp.logical_not(own) & (ps < 4))
            def _():
                for half in range(2):
                    kv_copy(
                        parray, 2 + j, ps, half,
                        jnp.where(j == 0, right_origin(ps), left_origin(ps)) + 1 - c, sib,
                    ).wait_recv()

            @pl.when(jnp.logical_not(own) & (ps == 4))
            def _():
                sib_wait(parray, 0, 4, 0)
                sib_wait(parray, 1, 4, 1)

            @pl.when((uarray == 1) | (chip < z))
            def _():
                attend(
                    pl.multiple_of(uarray * 2048 + chip * UNIT, UNIT),
                    jnp.where(uarray == 1, length - chip * UNIT, UNIT),
                    None,
                )

        return 0

    lax.fori_loop(0, 16, step, 0)
    sib_wait(1, 0, 4, 0)
    sib_wait(1, 1, 4, 1)
    final = lax.rem(z + 4, NZ)
    attend(pl.multiple_of(2048 + final * UNIT, UNIT), length - final * UNIT, None)
    for g in range(KVH):
        sums = acc[g]
        done = (sums[:, 0:DIM] / sums[:, DIM:2 * DIM]).astype(BF)
        for j in range(GRP):
            h = g * GRP + j
            att_ref[:, h * DIM:(h + 1) * DIM] = done[j * TOK:(j + 1) * TOK]

    for array in range(2):
        for half in range(2):
            kv_copy(array, 2, 0, half, me, sib).wait_send()
            for kind in range(2):
                last = 4 if half == kind else 3
                to = right if kind == 0 else left
                for s in range(1, last + 1):
                    kv_copy(array, kind, s, half, me, to).wait_send()
                    kv_copy(array, 2 + kind, s, half, me, sib).wait_send()

    def drain(k, _):
        pltpu.make_async_remote_copy(
            src_ref=reqs.at[mine], dst_ref=ids.at[mine],
            send_sem=isend.at[k], recv_sem=irecv.at[k],
            device_id=(me, lax.rem(ex + k, NEX)), device_id_type=MESH,
        ).wait_send()
        block_copy(k).wait_send()
        return 0

    lax.fori_loop(1, NEX, drain, 0)
    e_copy().wait_send()
    d_copy().wait_send()
    for k in range(NSUB):
        c_copy(k).wait_send()

        @pl.when(z < NZ - 1)
        def _():
            p_copy(k).wait_send()


def local(
    queries, new_kv, kv_pool, holders, slots, lengths,
    ssm_input, step_sizes, projections, decay_rates, skip_gain, init_state,
):
    kv = new_kv[0].reshape(TOK, 1024)
    pool = kv_pool.reshape(256, 1024)
    state = init_state[0].reshape(CH, STATE).T
    vmem = pl.BlockSpec(memory_space=pltpu.VMEM)
    smem = pl.BlockSpec(memory_space=pltpu.SMEM)
    dma = pltpu.SemaphoreType.DMA
    attended, ssm_out = pl.pallas_call(
        kernel,
        out_shape=(
            jax.ShapeDtypeStruct((TOK, 4096), BF),
            jax.ShapeDtypeStruct((TOK, CH), BF),
        ),
        in_specs=[vmem] * 5 + [smem] + [vmem] * 6,
        out_specs=(vmem, vmem),
        scratch_shapes=[
            pltpu.VMEM((32 * TOK, 1024), BF),
            pltpu.VMEM((KVH, GRP * TOK, DIM), BF),
            pltpu.VMEM((KVH, GRP * TOK, DIM), F32),
            pltpu.VMEM((KVH, GRP * TOK, 2 * DIM), F32),
            pltpu.VMEM((256, 128), I32),
            pltpu.VMEM((256, 128), I32),
            pltpu.VMEM((256, 1024), BF),
            pltpu.VMEM((256, 1024), BF),
            pltpu.VMEM((128, 256), BF),
            pltpu.VMEM((TOK, CH), BF),
            pltpu.VMEM((TOK, CH), F32),
            pltpu.VMEM((8, CH), F32),
            pltpu.VMEM((8, CH), F32),
            pltpu.VMEM((STATE, CH), F32),
            pltpu.VMEM((128, 128), BF),
            pltpu.VMEM((2, 128, 32), BF),
            pltpu.VMEM((STATE, HCH), BF),
            pltpu.VMEM((STATE, HCH), BF),
            pltpu.VMEM((8, HCH), F32),
            pltpu.VMEM((NSUB, STATE, SUB), BF),
            pltpu.VMEM((NSUB, STATE, SUB), BF),
            pltpu.VMEM((NSUB, STATE, SUB), BF),
            pltpu.VMEM((NSUB, STATE, SUB), BF),
            pltpu.VMEM((STATE, CH), F32),
            dma((80,)), dma((80,)),
            dma((NEX,)), dma((NEX,)),
            dma((NEX,)), dma((NEX,)),
            dma((2,)), dma((2,)),
            dma((NSUB,)), dma((NSUB,)),
            dma((NSUB,)), dma((NSUB,)),
        ],
        compiler_params=pltpu.CompilerParams(
            vmem_limit_bytes=58 * 2 ** 20, collective_id=3, has_side_effects=True
        ),
        name="resume",
    )(
        queries[0], kv, pool, holders, slots, lengths,
        ssm_input[0], step_sizes[0], projections[0],
        decay_rates[None], skip_gain[None], state,
    )
    return attended[None], ssm_out[None]


def solution(mesh):
    placed = (
        P("expert", "seq", None),
        P("expert", "seq", None, None),
        P(("seq", "expert"), None, None, None),
        P("expert", "seq"),
        P("expert", "seq"),
        P(),
        P("expert", "seq", None),
        P("expert", "seq", None),
        P("expert", "seq", None),
        P(),
        P(),
        P("expert", None, None),
    )
    return jax.shard_map(
        local,
        mesh=mesh,
        in_specs=placed,
        out_specs=(P("expert", "seq", None), P("expert", "seq", None)),
        check_vma=False,
    )
```

time: 260 us -> 96.7 us (0.37)
  matrix products: 94.8 us -> 0 us
  Pallas kernels: 0 us -> 81 us
  other arithmetic: 63.2 us -> 0 us
  blocking collectives: 36.4 us -> 0 us
  local copies, waits for them, and re-layouts: 36.3 us -> 13.4 us
  between operations: 14.1 us -> 0.65 us
  waiting for transfers between devices: 8.78 us -> 0 us
  starting transfers between devices: 3.83 us -> 0 us
    dot_general x12 -> x0, matrix products: 94.8 us -> none  [the longest x4 44.4 us: attend_block(): jnp.einsum('tkgs,skd->tkgd', weights.astype(jnp.bfloat16), value_rows, pr...]
    pallas_call x0 -> x1, Pallas kernels: none -> 81 us  [local(): pl.pallas_call(kernel, out_shape=(jax.ShapeDtypeStruct((TOK, 4096), BF),...]
    reduce_sum x6 -> x0, other arithmetic: 35.2 us -> none  [the longest x4 34.2 us: attend_block(): totals = totals * factor + jnp.sum(weights, axis=-1)]
    all_gather x1 -> x0, blocking collectives: 22.7 us -> none  [carried_in(): lax.all_gather(part.astype(kind), axis)]
    select_n x19 -> x0, other arithmetic: 19.8 us -> none  [the longest x16 17.5 us: step(): return jax.tree.map(lambda a, b: jnp.where(reached, a, b), new, before)]
    all_to_all x1 -> x0, blocking collectives: 13.8 us -> none  [local(): lax.all_to_all(requests, 'expert', split_axis=0, concat_axis=0, tiled=True)]
    all_to_all x1 -> x0, waiting for transfers between devices: 8.73 us -> none  [local(): lax.all_to_all(picked, 'expert', split_axis=0, concat_axis=0, tiled=True)]
    slice x5 -> x0, local copies, waits for them, and re-layouts: 8.72 us -> none  [the longest x4 8.71 us: attend_block(): value_rows = key_block[:, 1].reshape(key_count, kv_heads, head_depth)]
  transfers between devices with their start and end apart: 4 -> 0, of which waited for: 1 -> 0; matrix products, arithmetic and copies ran while one was open for 48% -> 0% of each run, Pallas kernels for 0% -> 0%
where the time goes in v1:
time: 96.7 us; the launch traced here: 95.1 us
  Pallas kernels  81 us (84%)
  local copies, waits for them, and re-layouts  13.4 us (14%)
    pallas_call x1, Pallas kernels, local(): pl.pallas_call(kernel, out_shape=(jax.ShapeDtypeStruct((TOK, 4096), BF),...  81 us
    another operation x2, local copies, waits for them, and re-layouts, local(): state = init_state[0].reshape(CH, STATE).T  7.29 us
    unnamed x13, local copies, waits for them, and re-layouts  6.11 us

profile of v1, /device:TPU:1, one launch (start us, length us, event | category | flops | bytes accessed | tf_op | source)
XLA Modules:
  0.0 95.1 jit_solution(15477923253939845895)
XLA Ops:
  0.6 3.7 %reshape_squeeze.7 = f32[8192,16]{1,0:T(8,128)} reshape(f32[1,128,1024]{2,1,0:T(8,128)} %param.23) | data formatting | bytes 1048576 | tf_op jit(solution)/shard_map/reshape;squeeze | solution.py:478
  4.3 0.0 copy-start.1
  4.3 0.0 copy-start.2
  4.3 0.0 copy-start.3
  4.3 3.6 %copy.16 = f32[8192,16]{0,1:T(8,128)} copy(f32[8192,16]{1,0:T(8,128)} %reshape_squeeze.7) | data formatting | bytes 1048576 | tf_op jit(solution)/shard_map/reshape;squeeze | solution.py:478
  7.9 0.0 copy-done.1
  7.9 0.9 copy.18
  8.8 0.0 copy-done.2
  8.8 0.7 copy.17
  9.5 0.0 copy-done.3
  9.5 0.7 copy.15
  10.3 81.0 %resume.1 = (bf16[128,4096]{1,0:T(8,128)(2,1)}, bf16[128,8192]{1,0:T(8,128)(2,1)}) custom-call(bf16[128,4096]{1,0:T(8,128)(2,1)} %bitcast.21, bf16[128,1024]{1,0:T(8,128)(2,1)} %bitcast.19, bf16[256,1024]{1,0:T(8,128)(2,1)} %bitcast.16, s32[1,16]{1,0:T(1,128)} %hold_ref.1, s32[1,16]{1,0:T(1,128)} %slot_ref.1, s32[16]{0:T(128)} %len_ref.1, ...), custom_call_target="tpu_custom_call" | custom-call | tf_op jit(solution)/shard_map/resume/pallas_call | solution.py:482
  91.3 0.0 copy-start
  91.3 2.4 %copy.21 = bf16[1,128,4096]{2,1,0:T(8,128)(2,1)} copy(bf16[1,128,4096]{2,1,0:T(8,128)(2,1)} %bitcast.20) | data formatting | bytes 2097152
  93.8 0.0 copy-done
  93.8 1.3 %copy.22 = bf16[1,128,8192]{2,1,0:T(8,128)(2,1)} copy(bf16[1,128,8192]{2,1,0:T(8,128)(2,1)S(1)} %bitcast.18) | data formatting | bytes 4194304
Async XLA Ops:
  4.3 3.6 %copy-start.1 = (bf16[32,8,2,512]{3,2,1,0:T(2,128)(2,1)S(1)}, bf16[32,8,2,512]{3,2,1,0:T(2,128)(2,1)}, u32[]{:S(2)}) copy-start(bf16[32,8,2,512]{3,2,1,0:T(2,128)(2,1)} %param.14) | copy-start | bytes 1572868
  4.3 4.5 %copy-start.2 = (bf16[1,128,2,512]{3,2,1,0:T(2,128)(2,1)S(1)}, bf16[1,128,2,512]{3,2,1,0:T(2,128)(2,1)}, u32[]{:S(2)}) copy-start(bf16[1,128,2,512]{3,2,1,0:T(2,128)(2,1)} %param.13) | copy-start | bytes 786436
  4.3 5.2 %copy-start.3 = (f32[1,128,32]{1,2,0:T(8,128)S(1)}, f32[1,128,32]{1,2,0:T(8,128)}, u32[]{:S(2)}) copy-start(f32[1,128,32]{1,2,0:T(8,128)} %param.20) | copy-start | bytes 49156
  91.3 2.4 %copy-start = (bf16[128,8192]{1,0:T(8,128)(2,1)S(1)}, bf16[128,8192]{1,0:T(8,128)(2,1)}, u32[]{:S(2)}) copy-start(bf16[128,8192]{1,0:T(8,128)(2,1)} %get-tuple-element.5) | copy-start | bytes 6291460

commit v2 on v1

v2 whole, which is shorter than its diff:
```python
import functools

import jax
import jax.numpy as jnp
from jax import lax
from jax.experimental import pallas as pl
from jax.experimental.pallas import tpu as pltpu
from jax.sharding import PartitionSpec as P

MESH = pl.DeviceIdType.MESH
BF = jnp.bfloat16
F32 = jnp.float32
I32 = jnp.int32
HIGH = lax.Precision.HIGHEST

KVH = 4
GRP = 8
DIM = 128
TOK = 128
NZ = 8
NEX = 16
READY = 9
SIDE = 4
UNIT = 256
HALF = 64
STATE = 16
CH = 8192
HCH = CH // 2
WIDE = 1024
NSUB = 2
SUB = HCH // NSUB
SCALE = (DIM ** -0.5) * 1.4426950408889634
LOW = -1e30


def iota(shape, axis):
    return lax.broadcasted_iota(I32, shape, axis)


def kernel(
    q_hbm, kv_ref, pool_hbm, hold_ref, slot_ref, len_ref,
    x_hbm, step_ref, proj_ref, decay_ref, skip_ref, init_hbm,
    att_hbm, ssm_hbm,
    q_ref, pool_ref, x_ref, init_ref, att_ref, ssm_ref,
    buf, qs, peak, acc, reqs, middle_ids, ids, picked, arrived, compact,
    xw, gain, dexp, sexp, ends, amat, plo,
    e_out, e_in, d_in, p_in, p_out, c_sib, c_in, carried,
    ksend, krecv, isend, irecv, bsend, brecv, esend, erecv, psend, precv, csend, crecv, lsend,
):
    me = lax.axis_index("seq")
    ex = lax.axis_index("expert")
    z = me // 2
    c = lax.rem(me, 2)
    right = lax.rem(z + 1, NZ) * 2 + c
    left = lax.rem(z + NZ - 1, NZ) * 2 + c
    sib = z * 2 + 1 - c

    barrier = pltpu.get_barrier_semaphore()
    for d in (right, left, sib):
        pl.semaphore_signal(barrier, inc=1, device_id=(d, ex), device_id_type=MESH)

    ey, exx = ex // SIDE, lax.rem(ex, SIDE)

    def along_y(k):
        return lax.rem(ex + SIDE * k, NEX)

    def along_x(k):
        return ey * SIDE + lax.rem(exx + k, SIDE)

    def greet(k, _):
        pl.semaphore_signal(
            barrier, inc=1, device_id=(me, along_y(k)), device_id_type=MESH
        )
        pl.semaphore_signal(
            barrier, inc=1, device_id=(me, along_x(k)), device_id_type=MESH
        )
        return 0

    lax.fori_loop(1, SIDE, greet, 0)

    x_load = pltpu.make_async_copy(x_hbm, x_ref, lsend.at[0])
    q_load = pltpu.make_async_copy(q_hbm, q_ref, lsend.at[1])
    pool_load = pltpu.make_async_copy(pool_hbm, pool_ref, lsend.at[2])
    init_load = pltpu.make_async_copy(init_hbm, init_ref, lsend.at[3])
    att_store = pltpu.make_async_copy(att_ref, att_hbm, lsend.at[4])
    ssm_store = pltpu.make_async_copy(ssm_ref, ssm_hbm, lsend.at[5])
    x_load.start()
    pool_load.start()
    q_load.start()

    @pl.when(z == 0)
    def _():
        init_load.start()

    def where_rows(array, origin, half):
        return pl.ds(pl.multiple_of((array * 16 + origin) * TOK + half * HALF, HALF), HALF)

    def kv_copy(array, kind, s, half, origin, to):
        k = ((array * 4 + kind) * 5 + s) * 2 + half
        ref = buf.at[where_rows(array, origin, half)]
        return pltpu.make_async_remote_copy(
            src_ref=ref, dst_ref=ref, send_sem=ksend.at[0], recv_sem=krecv.at[k],
            device_id=(to, ex), device_id_type=MESH,
        )

    def right_origin(s):
        return lax.rem(z + NZ - s, NZ) * 2

    def left_origin(s):
        return lax.rem(z + s, NZ) * 2

    def send_own(array):
        for half in range(2):
            kv_copy(array, 0, 1, half, me, right).start()
            kv_copy(array, 1, 1, half, me, left).start()
        for half in range(2):
            kv_copy(array, 2, 0, half, me, sib).start()

    buf[where_rows(0, me, 0)] = kv_ref[0:HALF]
    buf[where_rows(0, me, 1)] = kv_ref[HALF:TOK]

    spread = (iota((16, 128), 1) // 8 == iota((16, 128), 0)).astype(F32)
    hold = jnp.dot(hold_ref[...].astype(F32), spread, preferred_element_type=F32)
    slot = jnp.dot(slot_ref[...].astype(F32), spread, preferred_element_type=F32)
    row = iota((256, 128), 0)
    lane = iota((256, 128), 1)
    named = (hold[0:1] == (row // 16).astype(F32)).astype(F32)
    lead = ((iota((128, 128), 0) // 8 < iota((128, 128), 1) // 8)
            & (lax.rem(iota((128, 128), 0), 8) == 0)).astype(BF)
    before = jnp.dot(named.astype(BF), lead, preferred_element_type=F32)
    chosen = named * (before == lax.rem(row // 8, 2).astype(F32)).astype(F32)
    first = (lax.rem(lane, 8) == 0).astype(F32)
    wanted = jnp.sum(chosen * first * slot[0:1], axis=1, keepdims=True)
    reqs[...] = jnp.broadcast_to(wanted, (256, 128)).astype(I32).reshape(SIDE, 64, 128)
    place = chosen * (lax.rem(row, 8) == lax.rem(lane, 8)).astype(F32)
    compact[...] = place.T.astype(BF)

    pl.semaphore_wait(barrier, 9)
    send_own(0)


    def ask_y(k, _):
        to = along_y(k)
        pltpu.make_async_remote_copy(
            src_ref=reqs.at[to // SIDE], dst_ref=middle_ids.at[ey],
            send_sem=isend.at[0], recv_sem=irecv.at[0],
            device_id=(me, to), device_id_type=MESH,
        ).start()
        return 0

    lax.fori_loop(1, SIDE, ask_y, 0)
    middle_ids[ey] = reqs[ey]
    mine_x = pl.ds(pl.multiple_of(exx * 16, 16), 16)
    mine = pl.ds(pl.multiple_of(ex * 16, 16), 16)

    dec = decay_ref[...]
    steps = step_ref[...]
    lower = iota((128, 128), 0) >= iota((128, 128), 1)
    logs = jnp.dot(lower.astype(F32), -steps * dec, precision=HIGH, preferred_element_type=F32)
    total = logs[127:128]
    rows = jnp.concatenate(
        [
            jnp.exp(total - logs) * steps,
            jnp.exp(logs - total),
            jnp.broadcast_to(jnp.exp(total), (8, 128)),
            jnp.broadcast_to(skip_ref[...], (8, 128)),
        ],
        axis=0,
    )
    rows_hi = rows.astype(BF)
    rows_cat = jnp.concatenate([rows_hi, (rows - rows_hi.astype(F32)).astype(BF)], axis=1)
    proj_t = proj_ref[...]
    proj = proj_t.T
    write_t = jnp.concatenate([jnp.zeros((STATE, 128), F32), proj_t[0:STATE]], axis=0)
    affinity = jnp.dot(proj, write_t, precision=HIGH, preferred_element_type=F32)
    amat[...] = jnp.where(lower, affinity, 0.0).astype(BF)
    plo[0] = proj.astype(BF)
    plo[1] = (proj - proj.astype(BF).astype(F32)).astype(BF)
    pt_hi = proj_t.astype(BF)
    pt_lo = (proj_t - pt_hi.astype(F32)).astype(BF)

    x_load.wait()

    def widen(n, _):
        cols = pl.ds(pl.multiple_of(n * WIDE, WIDE), WIDE)
        one = (iota((128, WIDE), 0) == n * (WIDE // 64) + iota((128, WIDE), 1) // 64)
        one = one.astype(BF)
        wide = jnp.dot(
            rows_cat, jnp.concatenate([one, one], axis=0), preferred_element_type=F32
        )
        fed = (x_ref[:, cols].astype(F32) * wide[0:128]).astype(BF)
        xw[:, cols] = fed
        gain[:, cols] = wide[128:256]
        dexp[:, cols] = wide[256:264]
        sexp[:, cols] = wide[264:272]
        end = jnp.dot(pt_hi, fed, preferred_element_type=F32) + jnp.dot(
            pt_lo, fed, preferred_element_type=F32
        )
        ends[:, cols] = end[0:STATE]
        return 0

    widen(0, 0)
    widen(1, 0)
    my_half = pl.ds(pl.multiple_of(c * HCH, HCH), HCH)
    sib_half = pl.ds(pl.multiple_of((1 - c) * HCH, HCH), HCH)
    def e_copy():
        return pltpu.make_async_remote_copy(
            src_ref=e_out, dst_ref=e_in, send_sem=esend.at[0], recv_sem=erecv.at[0],
            device_id=(sib, ex), device_id_type=MESH,
        )

    def d_copy():
        return pltpu.make_async_remote_copy(
            src_ref=dexp.at[:, sib_half], dst_ref=d_in, send_sem=esend.at[1],
            recv_sem=erecv.at[1], device_id=(sib, ex), device_id_type=MESH,
        )

    def share_ends():
        e_out[...] = ends[:, sib_half].astype(BF)
        e_copy().start()
        d_copy().start()

    others = pl.ds(0, (NEX - 1) * 16)

    def ids_y():
        return pltpu.make_async_remote_copy(
            src_ref=reqs.at[pl.ds(0, SIDE - 1)], dst_ref=middle_ids.at[pl.ds(0, SIDE - 1)],
            send_sem=isend.at[0], recv_sem=irecv.at[0],
            device_id=(sib, ex), device_id_type=MESH,
        )

    def ids_x():
        part = pl.ds(0, 16 * (SIDE - 1))
        return pltpu.make_async_remote_copy(
            src_ref=middle_ids.at[:, part], dst_ref=ids.at[:, part],
            send_sem=isend.at[1], recv_sem=irecv.at[1],
            device_id=(sib, ex), device_id_type=MESH,
        )

    def blocks_all():
        return pltpu.make_async_remote_copy(
            src_ref=picked.at[others], dst_ref=arrived.at[others],
            send_sem=bsend.at[0], recv_sem=brecv.at[0],
            device_id=(sib, ex), device_id_type=MESH,
        )

    ids_y().wait_recv()

    def ask_x(k, _):
        to = along_x(k)
        part = pl.ds(pl.multiple_of(lax.rem(to, SIDE) * 16, 16), 16)
        pltpu.make_async_remote_copy(
            src_ref=middle_ids.at[:, part], dst_ref=ids.at[:, mine_x],
            send_sem=isend.at[1], recv_sem=irecv.at[1],
            device_id=(me, to), device_id_type=MESH,
        ).start()
        return 0

    lax.fori_loop(1, SIDE, ask_x, 0)
    ids[:, mine_x] = middle_ids[:, mine_x]
    q_load.wait()
    for g in range(KVH):
        for j in range(GRP):
            h = g * GRP + j
            qs[g, j * TOK:(j + 1) * TOK, :] = q_ref[:, h * DIM:(h + 1) * DIM]
    peak[...] = jnp.full_like(peak, LOW)
    acc[...] = jnp.zeros_like(acc)
    def hand_out():
        ids_x().wait_recv()
        got = ids[...].reshape(256, 128)
        same = lax.rem(row, 8) == lax.rem(lane, 8)
        pick = jnp.concatenate(
            [
                ((got == lane // 8) & same).astype(BF),
                ((got == lane // 8 + 16) & same).astype(BF),
            ],
            axis=1,
        )
        pool_load.wait()
        picked[...] = jnp.dot(pick, pool_ref[...], preferred_element_type=F32).astype(BF)
        arrived[mine] = picked[mine]

    def block_copy(k):
        to = lax.rem(ex + k, NEX)
        return pltpu.make_async_remote_copy(
            src_ref=picked.at[pl.ds(pl.multiple_of(to * 16, 16), 16)],
            dst_ref=arrived.at[pl.ds(pl.multiple_of(ex * 16, 16), 16)],
            send_sem=bsend.at[0], recv_sem=brecv.at[0],
            device_id=(me, to), device_id_type=MESH,
        )

    def give(k, _):
        block_copy(k).start()
        return 0

    length = len_ref[ex]

    def attend(start, shown, bias, heads):
        keep = iota((UNIT, DIM), 0) < shown
        one = keep.astype(F32).astype(BF)
        for g in heads:
            kcols = slice(g * DIM, (g + 1) * DIM)
            vcols = slice(512 + g * DIM, 512 + (g + 1) * DIM)
            key = buf[pl.ds(start, UNIT), kcols]
            value = buf[pl.ds(start, UNIT), vcols]
            key = jnp.where(keep, key, jnp.broadcast_to(kv_ref[0:1, kcols], (UNIT, DIM)))
            value = value * one
            score = lax.dot_general(
                qs[g], key, (((1,), (1,)), ((), ())), preferred_element_type=F32
            )
            if bias is not None:
                score = score + bias
            old = peak[g]
            new = jnp.maximum(old, jnp.max(score, axis=1, keepdims=True))
            weight = jnp.exp2((score - jnp.concatenate([new, new], 1)) * SCALE).astype(BF)
            factor = jnp.exp2((old - new) * SCALE)
            acc[g] = acc[g] * jnp.concatenate([factor, factor], 1) + jnp.dot(
                weight, jnp.concatenate([value, one], axis=1), preferred_element_type=F32
            )
            peak[g] = new

    def sib_wait(array, kind, s, half):
        if kind == 0:
            origin = right_origin(s)
        else:
            origin = left_origin(s)
        kv_copy(array, 2 + kind, s, half, origin + 1 - c, sib).wait_recv()

    def own_keys():
        for half in range(2):
            kv_copy(0, 2, 0, half, sib, sib).wait_recv()
        token = lax.rem(iota((GRP * TOK, UNIT), 0), TOK) + c * TOK
        bias = jnp.where(iota((GRP * TOK, UNIT), 1) <= token, 0.0, LOW)
        attend(pl.multiple_of(z * UNIT, UNIT), UNIT, bias, range(KVH))

    def p_copy(k):
        return pltpu.make_async_remote_copy(
            src_ref=p_out.at[k], dst_ref=p_in.at[k], send_sem=psend.at[k],
            recv_sem=precv.at[k], device_id=(right, ex), device_id_type=MESH,
        )

    def c_copy(k):
        return pltpu.make_async_remote_copy(
            src_ref=c_sib.at[k], dst_ref=c_in.at[k], send_sem=csend.at[k],
            recv_sem=crecv.at[k], device_id=(sib, ex), device_id_type=MESH,
        )

    def seed():
        init_load.wait()
        keep = lax.rem(iota((STATE, 2048), 1), STATE) == iota((STATE, 2048), 0)
        deep = iota((2048, 128), 0)
        move = (iota((2048, 128), 1) == lax.rem(deep, 1024) // STATE + 64 * (deep // 1024)).astype(BF)

        def batch(b, _):
            head = pl.multiple_of(c * 64 + b * 16, 16)
            heads = init_ref[pl.ds(head, 16), :]
            parts = []
            for i in range(8):
                pair = jnp.concatenate([heads[2 * i:2 * i + 1], heads[2 * i + 1:2 * i + 2]], axis=1)
                parts.append(jnp.where(keep, jnp.broadcast_to(pair, (STATE, 2048)), 0.0))
            full = jnp.concatenate(parts, axis=0)
            high = full.astype(BF)
            low = (full - high.astype(F32)).astype(BF)
            moved = jnp.dot(high, move, preferred_element_type=F32) + jnp.dot(
                low, move, preferred_element_type=F32
            )
            for i in range(8):
                carried[:, pl.ds(pl.multiple_of(head * 64 + i * 128, 128), 128)] = (
                    moved[i * STATE:(i + 1) * STATE]
                )
            return 0

        lax.fori_loop(0, 4, batch, 0)

    def chain():
        e_copy().wait_recv()
        d_copy().wait_recv()
        for k in range(NSUB):
            cols = pl.ds(pl.multiple_of(c * HCH + k * SUB, SUB), SUB)
            piece = slice(k * SUB, (k + 1) * SUB)

            @pl.when(z > 0)
            def _():
                p_copy(k).wait_recv()
                carried[:, cols] = p_in[k].astype(F32)

            @pl.when(z == 0)
            def _():
                if k == 0:
                    seed()

            entering = carried[:, cols]
            own_e, own_d = ends[:, cols], dexp[0:1, cols]
            sib_e, sib_d = e_in[:, piece].astype(F32), d_in[0:1, piece]
            even = c == 0
            e0, e1 = jnp.where(even, own_e, sib_e), jnp.where(even, sib_e, own_e)
            d0, d1 = jnp.where(even, own_d, sib_d), jnp.where(even, sib_d, own_d)
            middle = d0 * entering + e0
            p_out[k] = (d1 * middle + e1).astype(BF)

            @pl.when(z < NZ - 1)
            def _():
                p_copy(k).start()

            c_sib[k] = jnp.where(even, middle, entering).astype(BF)
            c_copy(k).start()
            carried[:, cols] = jnp.where(even, entering, middle)

    def ssm_ready():
        for k in range(NSUB):
            c_copy(k).wait_recv()
            cols = pl.ds(pl.multiple_of((1 - c) * HCH + k * SUB, SUB), SUB)
            carried[:, cols] = c_in[k].astype(F32)

    def ssm_finish(n):
        cols = pl.ds(pl.multiple_of(n * WIDE, WIDE), WIDE)
        state = (carried[:, cols] * dexp[0:1, cols]).astype(BF)
        state = jnp.concatenate([jnp.zeros((STATE, WIDE), BF), state], axis=0)
        mixed = (
            jnp.dot(amat[...], xw[:, cols], preferred_element_type=F32)
            + jnp.dot(plo[0], state, preferred_element_type=F32)
            + jnp.dot(plo[1], state, preferred_element_type=F32)
        )
        ssm_ref[:, cols] = (
            gain[:, cols] * mixed + sexp[0:1, cols] * x_ref[:, cols].astype(F32)
        ).astype(BF)

    def assemble():
        blocks_all().wait_recv()
        context = jnp.dot(compact[...], arrived[...], preferred_element_type=F32).astype(BF)
        buf[where_rows(1, me, 0)] = context[0:HALF]
        buf[where_rows(1, me, 1)] = context[HALF:TOK]
        send_own(1)

    def stage(k):
        is_ctx = (k == 3) | (k >= 5)
        s = jnp.where(k < 3, k + 1, jnp.where(k == 3, 1, jnp.where(k == 4, 4, k - 3)))
        return jnp.where(is_ctx, 1, 0), s

    turn = 8 + (18 * z) // 7

    def step(fine, _):
        it = fine // 2
        kind = lax.rem(fine, 2)
        early = kind == 0
        k = it // 2
        j = lax.rem(it, 2)
        array, s = stage(k)
        last = 4 - j

        @pl.when(fine == READY)
        def _():
            assemble()

        @pl.when(s <= last)
        def _():
            half = jnp.where(early, j, 1 - j)
            origin = jnp.where(early, right_origin(s), left_origin(s)) + c
            kv_copy(array, kind, s, half, origin, sib).wait_recv()

            @pl.when(s < last)
            def _():
                kv_copy(array, kind, s + 1, half, origin, jnp.where(early, right, left)).start()

            kv_copy(array, 2 + kind, s, half, origin, sib).start()

        @pl.when(fine == 1)
        def _():
            hand_out()

        @pl.when((fine >= 1) & (fine <= 3))
        def _():
            lax.fori_loop(5 * fine - 4, 5 * fine + 1, give, 0)

        @pl.when((fine <= 6) & (fine != 1))
        def _():
            widen(jnp.where(fine == 0, 2, fine + 1), 0)

        @pl.when(fine == 6)
        def _():
            share_ends()

        @pl.when(fine == 7)
        def _():
            own_keys()

        @pl.when(fine == turn)
        def _():
            chain()

        @pl.when(fine == turn + 3)
        def _():
            ssm_ready()

        @pl.when((fine >= turn + 3) & (fine < turn + 3 + CH // WIDE))
        def _():
            ssm_finish(fine - turn - 3)

        parray, ps = stage(k - 1)
        own = (k - 1 == 4) & (j == 1)
        uarray = jnp.where(own, 1, parray)
        chip = jnp.where(
            own, z, lax.rem(jnp.where(j == 0, z + NZ - ps, z + ps), NZ)
        )

        @pl.when(it >= 2)
        def _():
            @pl.when(own & early)
            def _():
                for half in range(2):
                    kv_copy(1, 2, 0, half, sib, sib).wait_recv()

            @pl.when(jnp.logical_not(own) & (ps < 4) & early)
            def _():
                for half in range(2):
                    kv_copy(
                        parray, 2 + j, ps, half,
                        jnp.where(j == 0, right_origin(ps), left_origin(ps)) + 1 - c, sib,
                    ).wait_recv()

            @pl.when(jnp.logical_not(own) & (ps == 4) & early)
            def _():
                sib_wait(parray, 0, 4, 0)
                sib_wait(parray, 1, 4, 1)

            for part in range(2):

                @pl.when(((uarray == 1) | (chip < z)) & (kind == part))
                def _():
                    attend(
                        pl.multiple_of(uarray * 2048 + chip * UNIT, UNIT),
                        jnp.where(uarray == 1, length - chip * UNIT, UNIT),
                        None,
                        (2 * part, 2 * part + 1),
                    )

        return 0

    lax.fori_loop(0, 32, step, 0)

    def rest(n, _):
        ssm_finish(n)
        return 0

    lax.fori_loop(jnp.minimum(CH // WIDE, 32 - turn - 3), CH // WIDE, rest, 0)
    ssm_store.start()
    sib_wait(1, 0, 4, 0)
    sib_wait(1, 1, 4, 1)
    final = lax.rem(z + 4, NZ)
    attend(pl.multiple_of(2048 + final * UNIT, UNIT), length - final * UNIT, None, range(KVH))
    for g in range(KVH):
        sums = acc[g]
        done = (sums[:, 0:DIM] / sums[:, DIM:2 * DIM]).astype(BF)
        for j in range(GRP):
            h = g * GRP + j
            att_ref[:, h * DIM:(h + 1) * DIM] = done[j * TOK:(j + 1) * TOK]

    att_store.start()

    sent = buf.at[pl.ds(0, 60 * HALF)]
    pltpu.make_async_remote_copy(
        src_ref=sent, dst_ref=sent, send_sem=ksend.at[0], recv_sem=krecv.at[0],
        device_id=(sib, ex), device_id_type=MESH,
    ).wait_send()
    ids_y().wait_send()
    ids_x().wait_send()
    blocks_all().wait_send()
    e_copy().wait_send()
    d_copy().wait_send()
    ssm_store.wait()
    att_store.wait()
    for k in range(NSUB):
        c_copy(k).wait_send()

        @pl.when(z < NZ - 1)
        def _():
            p_copy(k).wait_send()


def local(
    queries, new_kv, kv_pool, holders, slots, lengths,
    ssm_input, step_sizes, projections, decay_rates, skip_gain, init_state,
):
    kv = new_kv[0].reshape(TOK, 1024)
    pool = kv_pool.reshape(256, 1024)
    vmem = pl.BlockSpec(memory_space=pltpu.VMEM)
    far = pl.BlockSpec(memory_space=pl.ANY)
    smem = pl.BlockSpec(memory_space=pltpu.SMEM)
    dma = pltpu.SemaphoreType.DMA
    attended, ssm_out = pl.pallas_call(
        kernel,
        out_shape=(
            jax.ShapeDtypeStruct((TOK, 4096), BF),
            jax.ShapeDtypeStruct((TOK, CH), BF),
        ),
        in_specs=[far, vmem, far, vmem, vmem, smem, far] + [vmem] * 4 + [far],
        out_specs=(far, far),
        scratch_shapes=[
            pltpu.VMEM((TOK, 4096), BF),
            pltpu.VMEM((256, 1024), BF),
            pltpu.VMEM((TOK, CH), BF),
            pltpu.VMEM((128, 1024), F32),
            pltpu.VMEM((TOK, 4096), BF),
            pltpu.VMEM((TOK, CH), BF),
            pltpu.VMEM((32 * TOK, 1024), BF),
            pltpu.VMEM((KVH, GRP * TOK, DIM), BF),
            pltpu.VMEM((KVH, GRP * TOK, DIM), F32),
            pltpu.VMEM((KVH, GRP * TOK, 2 * DIM), F32),
            pltpu.VMEM((SIDE, 64, 128), I32),
            pltpu.VMEM((SIDE, 64, 128), I32),
            pltpu.VMEM((SIDE, 64, 128), I32),
            pltpu.VMEM((256, 1024), BF),
            pltpu.VMEM((256, 1024), BF),
            pltpu.VMEM((128, 256), BF),
            pltpu.VMEM((TOK, CH), BF),
            pltpu.VMEM((TOK, CH), F32),
            pltpu.VMEM((8, CH), F32),
            pltpu.VMEM((8, CH), F32),
            pltpu.VMEM((STATE, CH), F32),
            pltpu.VMEM((128, 128), BF),
            pltpu.VMEM((2, 128, 32), BF),
            pltpu.VMEM((STATE, HCH), BF),
            pltpu.VMEM((STATE, HCH), BF),
            pltpu.VMEM((8, HCH), F32),
            pltpu.VMEM((NSUB, STATE, SUB), BF),
            pltpu.VMEM((NSUB, STATE, SUB), BF),
            pltpu.VMEM((NSUB, STATE, SUB), BF),
            pltpu.VMEM((NSUB, STATE, SUB), BF),
            pltpu.VMEM((STATE, CH), F32),
            dma((1,)), dma((80,)),
            dma((2,)), dma((2,)),
            dma((1,)), dma((1,)),
            dma((2,)), dma((2,)),
            dma((NSUB,)), dma((NSUB,)),
            dma((NSUB,)), dma((NSUB,)),
            dma((6,)),
        ],
        compiler_params=pltpu.CompilerParams(
            vmem_limit_bytes=58 * 2 ** 20, collective_id=3, has_side_effects=True
        ),
        name="resume",
    )(
        queries[0], kv, pool, holders, slots, lengths,
        ssm_input[0], step_sizes[0], projections[0].T,
        decay_rates[None], skip_gain[None], init_state[0],
    )
    return attended[None], ssm_out[None]


def solution(mesh):
    placed = (
        P("expert", "seq", None),
        P("expert", "seq", None, None),
        P(("seq", "expert"), None, None, None),
        P("expert", "seq"),
        P("expert", "seq"),
        P(),
        P("expert", "seq", None),
        P("expert", "seq", None),
        P("expert", "seq", None),
        P(),
        P(),
        P("expert", None, None),
    )
    return jax.shard_map(
        local,
        mesh=mesh,
        in_specs=placed,
        out_specs=(P("expert", "seq", None), P("expert", "seq", None)),
        check_vma=False,
    )
```

time: 96.7 us -> 73.8 us (0.76)
  the two profiles are of different devices: /device:TPU:1 before, /device:TPU:192 now
where the time goes in v2:
time: 73.8 us; the launch traced here: 73.7 us
  Pallas kernels  65.7 us (89%)
  local copies, waits for them, and re-layouts  7.36 us (10%)
    pallas_call x1, Pallas kernels, local(): pl.pallas_call(kernel, out_shape=(jax.ShapeDtypeStruct((TOK, 4096), BF),...  65.7 us
    unnamed x6, local copies, waits for them, and re-layouts  7.36 us

profile of v2, /device:TPU:192, one launch (start us, length us, event | category | flops | bytes accessed | tf_op | source)
XLA Modules:
  0.0 73.7 jit_solution(14100524535974687847)
XLA Ops:
  0.6 1.7 %copy.14 = bf16[16,8,2,512]{3,1,2,0:T(8,128)(2,1)} copy(bf16[16,8,2,512]{3,2,1,0:T(2,128)(2,1)} %bitcast.24) | data formatting | bytes 524288
  2.3 1.9 %copy.15 = bf16[32,8,2,512]{3,1,2,0:T(8,128)(2,1)} copy(bf16[32,8,2,512]{3,2,1,0:T(2,128)(2,1)} %param.14) | data formatting | bytes 1048576
  4.2 65.7 %resume.1 = (bf16[128,4096]{1,0:T(8,128)(2,1)}, bf16[128,8192]{1,0:T(8,128)(2,1)}) custom-call(bf16[128,4096]{1,0:T(8,128)(2,1)} %bitcast.22, bf16[128,1024]{1,0:T(8,128)(2,1)} %bitcast.20, bf16[256,1024]{1,0:T(8,128)(2,1)} %bitcast.17, s32[1,16]{1,0:T(1,128)} %hold_ref.1, s32[1,16]{1,0:T(1,128)} %slot_ref.1, s32[16]{0:T(128)} %len_ref.1, ...), custom_call_target="tpu_custom_call" | custom-call | tf_op jit(solution)/shard_map/resume/pallas_call | solution.py:590
  69.9 0.0 copy-start
  69.9 2.4 %copy.18 = bf16[1,128,4096]{2,1,0:T(8,128)(2,1)} copy(bf16[1,128,4096]{2,1,0:T(8,128)(2,1)} %bitcast.21) | data formatting | bytes 2097152
  72.3 0.0 copy-done
  72.3 1.3 %copy.19 = bf16[1,128,8192]{2,1,0:T(8,128)(2,1)} copy(bf16[1,128,8192]{2,1,0:T(8,128)(2,1)S(1)} %bitcast.19) | data formatting | bytes 4194304
Async XLA Ops:
  69.9 2.4 %copy-start = (bf16[128,8192]{1,0:T(8,128)(2,1)S(1)}, bf16[128,8192]{1,0:T(8,128)(2,1)}, u32[]{:S(2)}) copy-start(bf16[128,8192]{1,0:T(8,128)(2,1)} %get-tuple-element.5) | copy-start | bytes 6291460

commit v3 on v2

--- a/solution.py
+++ b/solution.py
@@ -38,10 +38,10 @@
 
 
 def kernel(
-    q_hbm, kv_ref, pool_hbm, hold_ref, slot_ref, len_ref,
+    q_hbm, kv_both, pool_hbm, hold_ref, slot_ref, len_ref,
     x_hbm, step_ref, proj_ref, decay_ref, skip_ref, init_hbm,
     att_hbm, ssm_hbm,
-    q_ref, pool_ref, x_ref, init_ref, att_ref, ssm_ref,
+    q_ref, pool_both, kv_ref, pool_ref, x_ref, init_ref, att_ref, ssm_ref,
     buf, qs, peak, acc, reqs, middle_ids, ids, picked, arrived, compact,
     xw, gain, dexp, sexp, ends, amat, plo,
     e_out, e_in, d_in, p_in, p_out, c_sib, c_in, carried,
@@ -80,7 +80,7 @@
 
     x_load = pltpu.make_async_copy(x_hbm, x_ref, lsend.at[0])
     q_load = pltpu.make_async_copy(q_hbm, q_ref, lsend.at[1])
-    pool_load = pltpu.make_async_copy(pool_hbm, pool_ref, lsend.at[2])
+    pool_load = pltpu.make_async_copy(pool_hbm, pool_both, lsend.at[2])
     init_load = pltpu.make_async_copy(init_hbm, init_ref, lsend.at[3])
     att_store = pltpu.make_async_copy(att_ref, att_hbm, lsend.at[4])
     ssm_store = pltpu.make_async_copy(ssm_ref, ssm_hbm, lsend.at[5])
@@ -116,6 +116,8 @@
         for half in range(2):
             kv_copy(array, 2, 0, half, me, sib).start()
 
+    kv_ref[:, 0:512] = kv_both[:, 0, :]
+    kv_ref[:, 512:1024] = kv_both[:, 1, :]
     buf[where_rows(0, me, 0)] = kv_ref[0:HALF]
     buf[where_rows(0, me, 1)] = kv_ref[HALF:TOK]
 
@@ -277,6 +279,8 @@
             axis=1,
         )
         pool_load.wait()
+        pool_ref[:, 0:512] = pool_both[:, 0, :]
+        pool_ref[:, 512:1024] = pool_both[:, 1, :]
         picked[...] = jnp.dot(pick, pool_ref[...], preferred_element_type=F32).astype(BF)
         arrived[mine] = picked[mine]
 
@@ -581,8 +585,8 @@
     queries, new_kv, kv_pool, holders, slots, lengths,
     ssm_input, step_sizes, projections, decay_rates, skip_gain, init_state,
 ):
-    kv = new_kv[0].reshape(TOK, 1024)
-    pool = kv_pool.reshape(256, 1024)
+    kv = new_kv[0]
+    pool = kv_pool.reshape(256, 2, 512)
     vmem = pl.BlockSpec(memory_space=pltpu.VMEM)
     far = pl.BlockSpec(memory_space=pl.ANY)
     smem = pl.BlockSpec(memory_space=pltpu.SMEM)
@@ -597,6 +601,8 @@
         out_specs=(far, far),
         scratch_shapes=[
             pltpu.VMEM((TOK, 4096), BF),
+            pltpu.VMEM((256, 2, 512), BF),
+            pltpu.VMEM((TOK, 1024), BF),
             pltpu.VMEM((256, 1024), BF),
             pltpu.VMEM((TOK, CH), BF),
             pltpu.VMEM((128, 1024), F32),

time: 73.8 us -> 70.6 us (0.957)
  the two profiles are of different devices: /device:TPU:192 before, /device:TPU:196 now
where the time goes in v3:
time: 70.6 us; the launch traced here: 70.5 us
  Pallas kernels  66.1 us (94%)
  local copies, waits for them, and re-layouts  3.76 us (5%)
    pallas_call x1, Pallas kernels, local(): pl.pallas_call(kernel, out_shape=(jax.ShapeDtypeStruct((TOK, 4096), BF),...  66.1 us
    unnamed x4, local copies, waits for them, and re-layouts  3.76 us

profile of v3, /device:TPU:196, one launch (start us, length us, event | category | flops | bytes accessed | tf_op | source)
XLA Modules:
  0.0 70.5 jit_solution(36437020291587000)
XLA Ops:
  0.6 66.1 %resume.1 = (bf16[128,4096]{1,0:T(8,128)(2,1)}, bf16[128,8192]{1,0:T(8,128)(2,1)}) custom-call(bf16[128,4096]{1,0:T(8,128)(2,1)} %bitcast.16, bf16[128,2,512]{2,1,0:T(2,128)(2,1)} %bitcast.19, bf16[256,2,512]{2,1,0:T(2,128)(2,1)} %bitcast.17, s32[1,16]{1,0:T(1,128)} %hold_ref.1, s32[1,16]{1,0:T(1,128)} %slot_ref.1, s32[16]{0:T(128)} %len_ref.1, ...), custom_call_target="tpu_custom_call" | custom-call | tf_op jit(solution)/shard_map/resume/pallas_call | solution.py:594
  66.7 0.0 copy-start
  66.7 2.4 %copy.16 = bf16[1,128,4096]{2,1,0:T(8,128)(2,1)} copy(bf16[1,128,4096]{2,1,0:T(8,128)(2,1)} %bitcast.15) | data formatting | bytes 2097152
  69.2 0.0 copy-done
  69.2 1.3 %copy.17 = bf16[1,128,8192]{2,1,0:T(8,128)(2,1)} copy(bf16[1,128,8192]{2,1,0:T(8,128)(2,1)S(1)} %bitcast.14) | data formatting | bytes 4194304
Async XLA Ops:
  66.7 2.4 %copy-start = (bf16[128,8192]{1,0:T(8,128)(2,1)S(1)}, bf16[128,8192]{1,0:T(8,128)(2,1)}, u32[]{:S(2)}) copy-start(bf16[128,8192]{1,0:T(8,128)(2,1)} %get-tuple-element.5) | copy-start | bytes 6291460

commit v4 on v3

--- a/solution.py
+++ b/solution.py
@@ -450,15 +450,16 @@
         k = it // 2
         j = lax.rem(it, 2)
         array, s = stage(k)
-        last = 4 - j
+        turned = jnp.where(s == 4, 1 - j, j)
+        last = 4 - turned
 
         @pl.when(fine == READY)
         def _():
             assemble()
 
-        @pl.when(s <= last)
-        def _():
-            half = jnp.where(early, j, 1 - j)
+        @pl.when((s <= last) & (k < 7))
+        def _():
+            half = jnp.where(early, turned, 1 - turned)
             origin = jnp.where(early, right_origin(s), left_origin(s)) + c
             kv_copy(array, kind, s, half, origin, sib).wait_recv()
 
@@ -541,6 +542,11 @@
         return 0
 
     lax.fori_loop(0, 32, step, 0)
+
+    for kind in range(2):
+        origin = (right_origin(4) if kind == 0 else left_origin(4)) + c
+        kv_copy(1, kind, 4, kind, origin, sib).wait_recv()
+        kv_copy(1, 2 + kind, 4, kind, origin, sib).start()
 
     def rest(n, _):
         ssm_finish(n)

time: 70.6 us -> 71.6 us (1.014)
  the two profiles are of different devices: /device:TPU:196 before, /device:TPU:1 now
where the time goes in v4:
time: 71.6 us; the launch traced here: 70.7 us
  Pallas kernels  66.3 us (93%)
  local copies, waits for them, and re-layouts  3.76 us (5%)
    pallas_call x1, Pallas kernels, local(): pl.pallas_call(kernel, out_shape=(jax.ShapeDtypeStruct((TOK, 4096), BF),...  66.3 us
    unnamed x4, local copies, waits for them, and re-layouts  3.76 us

profile of v4, /device:TPU:1, one launch (start us, length us, event | category | flops | bytes accessed | tf_op | source)
XLA Modules:
  0.0 70.7 jit_solution(4101115277086726339)
XLA Ops:
  0.6 66.3 %resume.1 = (bf16[128,4096]{1,0:T(8,128)(2,1)}, bf16[128,8192]{1,0:T(8,128)(2,1)}) custom-call(bf16[128,4096]{1,0:T(8,128)(2,1)} %bitcast.16, bf16[128,2,512]{2,1,0:T(2,128)(2,1)} %bitcast.19, bf16[256,2,512]{2,1,0:T(2,128)(2,1)} %bitcast.17, s32[1,16]{1,0:T(1,128)} %hold_ref.1, s32[1,16]{1,0:T(1,128)} %slot_ref.1, s32[16]{0:T(128)} %len_ref.1, ...), custom_call_target="tpu_custom_call" | custom-call | tf_op jit(solution)/shard_map/resume/pallas_call | solution.py:600
  66.9 0.0 copy-start
  66.9 2.4 %copy.16 = bf16[1,128,4096]{2,1,0:T(8,128)(2,1)} copy(bf16[1,128,4096]{2,1,0:T(8,128)(2,1)} %bitcast.15) | data formatting | bytes 2097152
  69.4 0.0 copy-done
  69.4 1.3 %copy.17 = bf16[1,128,8192]{2,1,0:T(8,128)(2,1)} copy(bf16[1,128,8192]{2,1,0:T(8,128)(2,1)S(1)} %bitcast.14) | data formatting | bytes 4194304
Async XLA Ops:
  66.9 2.4 %copy-start = (bf16[128,8192]{1,0:T(8,128)(2,1)S(1)}, bf16[128,8192]{1,0:T(8,128)(2,1)}, u32[]{:S(2)}) copy-start(bf16[128,8192]{1,0:T(8,128)(2,1)} %get-tuple-element.5) | copy-start | bytes 6291460
